TPU v7x, 32 devices: a whole 2x2x4 slice. The times are simulated.
32 devices in a mesh: groups: 2 (over y), sx: 4 (over z), sy: 2 (over x), sz: 2 (over core).
Axes of the slice: x: 2, y: 2, z: 4, core: 2. Of those that a mesh axis runs over, the one named last changes fastest.
Arguments:
- prior: float32 [128, 32, 16, 256], P(None, ('groups', 'sx'), ('sy', 'sz')), parts along dimension 1, may hold values from -6 to 6
- current: float32 [64, 32, 16, 256], P(None, ('groups', 'sx'), ('sy', 'sz')), parts along dimension 1, may hold values from -150 to 150
- site_xy: float32 [2, 32, 16, 256], P(None, ('groups', 'sx'), ('sy', 'sz')), parts along dimension 1, may hold values from 0 to 1
- links: int32 [9, 32, 16], P(None, ('groups', 'sx'), ('sy', 'sz')), parts along dimension 1, may hold values from 0 to 1, as said below
Outputs:
- first_block: float32 [64, 32, 16, 256], P(None, ('groups', 'sx'), ('sy', 'sz')), parts along dimension 1
- second_block: float32 [64, 32, 16, 256], P(None, ('groups', 'sx'), ('sy', 'sz')), parts along dimension 1
There are 2 independent parts, one for each index of `groups`. A program takes and returns all parts, laid end to end along the dimension named above; each array names one. Nothing has to cross between parts.
Inputs may be any that keep to these rules, and one draw needn't show every extreme that they name: links[o] of a tile equals links[8 - o] of the tile it points to; links[4] is 1; links that point out of the grid are 0.
All inputs are finite; a program needn't handle non-finite values.
Results may differ from a plain program's by a relative error of at most 0.00027.
Values sent between devices are 32-bit elements; how exact they have to be, the bound alone decides.
A program may use at most 64 MiB of HBM per device.

v0:
```python
import jax
import jax.numpy as jnp
from jax import lax
from jax.sharding import PartitionSpec as P

kernel_gain = 0.0625


def extended(block, sides, width):
    for axis, dim in sides:
        count = lax.axis_size(axis)
        forward = [(i, i + 1) for i in range(count - 1)]
        backward = [(target, source) for source, target in forward]
        low = lax.ppermute(
            lax.slice_in_dim(block, block.shape[dim] - width, None, axis=dim), axis, forward
        )
        high = lax.ppermute(lax.slice_in_dim(block, 0, width, axis=dim), axis, backward)
        block = jnp.concatenate([low, block, high], axis=dim)
    return block


def lower_solve(lower, rhs):
    return lax.linalg.triangular_solve(lower, rhs, left_side=True, lower=True)


def kernel_weights(own, near, shift_x, shift_y, link):
    delta_x = own[0][..., :, None] - near[0][..., None, :] - shift_x
    delta_y = own[1][..., :, None] - near[1][..., None, :] - shift_y
    dist = jnp.sqrt(delta_x * delta_x + delta_y * delta_y)
    fall = jnp.maximum(1.0 - dist, 0.0)
    return fall**4 * (4.0 * dist + 1.0) * kernel_gain * link[..., None, None]


def build_weights(places, link_f):
    tiles_x = places.shape[1]
    tiles_y = places.shape[2]
    padded = extended(places, (("sx", 1), (("sy", "sz"), 2)), 1)
    tables = []
    for code in range(9):
        shift_x = code // 3 - 1
        shift_y = code % 3 - 1
        near = padded[:, 1 + shift_x : 1 + shift_x + tiles_x, 1 + shift_y : 1 + shift_y + tiles_y]
        tables.append(kernel_weights(places, near, shift_x, shift_y, link_f[code]))
    return jnp.stack(tables, axis=0)


def coupling(total, padded, weights, code):
    tiles_x = weights.shape[1]
    tiles_y = weights.shape[2]
    shift_x = code // 3 - 1
    shift_y = code % 3 - 1
    near = padded[:, 1 + shift_x : 1 + shift_x + tiles_x, 1 + shift_y : 1 + shift_y + tiles_y]
    return total + jnp.einsum(
        "xyij,mxyj->mxyi", weights[code], near, precision=lax.Precision.HIGHEST
    )


def apply_kernel(block, weights):
    total = jnp.zeros(block.shape, jnp.float32)
    codes = list(range(9))
    padded = extended(block, (("sx", 1), (("sy", "sz"), 2)), 1)
    for code in codes:
        total = coupling(total, padded, weights, code)
    return total


def inner(left, right):
    return lax.dot_general(
        left,
        right,
        (((1,), (1,)), ((), ())),
        precision=lax.Precision.HIGHEST,
        preferred_element_type=jnp.float32,
    )


def matmul(left, right):
    return jnp.dot(left, right, precision=lax.Precision.HIGHEST, preferred_element_type=jnp.float32)


def on_device(prior, current, site_xy, links):
    sites_total = float(
        prior.shape[1]
        * prior.shape[2]
        * prior.shape[3]
        * lax.axis_size("sx")
        * lax.axis_size("sy")
        * lax.axis_size("sz")
    )
    link_f = links.astype(jnp.float32)
    weights = build_weights(site_xy, link_f)
    width = current.shape[0]

    def lanczos_step(flat_span, block):
        flat_image = apply_kernel(block, weights).reshape(width, -1)
        coef = lax.psum(inner(flat_span, flat_image), ("sx", "sy", "sz")) / sites_total
        flat_image = flat_image - matmul(coef.T, flat_span)
        gram = lax.psum(inner(flat_image, flat_image), ("sx", "sy", "sz")) / sites_total
        lower = jnp.linalg.cholesky(gram)
        return lower_solve(lower, flat_image)

    span = jnp.concatenate([prior, current], axis=0)
    flat_span = span.reshape(span.shape[0], -1)
    flat_first = lanczos_step(flat_span, current)
    first_block = flat_first.reshape(current.shape)
    flat_span = jnp.concatenate([flat_span, flat_first], axis=0)
    second_block = lanczos_step(flat_span, first_block).reshape(current.shape)
    return (first_block, second_block)


def solution(mesh):
    return jax.shard_map(
        on_device,
        mesh=mesh,
        in_specs=(
            P(None, ("groups", "sx"), ("sy", "sz"), None),
            P(None, ("groups", "sx"), ("sy", "sz"), None),
            P(None, ("groups", "sx"), ("sy", "sz"), None),
            P(None, ("groups", "sx"), ("sy", "sz")),
        ),
        out_specs=(
            P(None, ("groups", "sx"), ("sy", "sz"), None),
            P(None, ("groups", "sx"), ("sy", "sz"), None),
        ),
        check_vma=False,
    )
```

profile of v0, /device:TPU:0, one launch (start us, length us, event | category | flops | bytes accessed | tf_op | source)
XLA Modules:
  0.0 531.8 jit_solution(18305448948203368599)
XLA Ops:
  7.2 0.9 fusion.347
  8.1 4.9 collective-permute-start.3
  13.0 1.3 collective-permute-start.4
  14.3 1.8 copy.22
  16.2 0.8 fusion.345
  17.0 4.7 collective-permute-start
  21.7 1.3 collective-permute-start.1
  23.1 0.8 fusion.250
  23.9 1.8 constant_dynamic-update-slice_fusion.11
  25.6 8.3 %fusion.179 = f32[64,4,4,256]{3,0,2,1:T(8,128)} fusion(f32[4,4]{1,0:T(4,128)S(1)} %get-tuple-element.8, f32[4,4,256]{2,1,0:T(4,128)S(1)} %get-tuple-element.43, f32[4,4,256]{2,1,0:T(4,128)S(1)} %get-tuple-element.42, f32[64,4,4,256]{3,2,1,0:T(4,128)S(1)} %copy-done.2), kind=kOutput, calls=%fused_computation.195 | convolution fusion | flops 818937856 | bytes 2129984 | tf_op jit(solution)/shard_map/xyij,mxyj->mxyi/dot_general | solution.py:53
  34.0 1.2 constant_dynamic-update-slice_fusion.10
  35.1 3.5 reshape.78
  38.8 1.4 collective-permute-start.7
  40.3 3.0 collective-permute-start.5
  44.2 1.8 constant_dynamic-update-slice_fusion.1
  46.1 1.0 constant_dynamic-update-slice_fusion
  47.1 1.3 collective-permute-start.6
  48.4 3.7 collective-permute-start.2
  52.1 8.1 %fusion.177 = f32[64,4,4,256]{3,0,2,1:T(8,128)S(1)} fusion(f32[4,4]{1,0:T(4,128)S(1)} %copy-done.37, f32[4,4,256]{2,1,0:T(4,128)S(1)} %get-tuple-element.38, f32[4,4,256]{2,1,0:T(4,128)S(1)} %get-tuple-element.37, f32[4,4,256]{2,1,0:T(4,128)S(1)} %copy-done.18, f32[4,4,256]{2,1,0:T(4,128)S(1)} %copy-done.15, f32[64,1,4,256]{3,0,2,1:T(8,128)} %collective-permute-done.1, ...), kind=kOutput, calls=%fused_computation.193 | convolution fusion | flops 820314112 | bytes 2424896 | tf_op jit(solution)/shard_map/xyij,mxyj->mxyi/dot_general | solution.py:53
  60.3 7.4 %fusion.10 = f32[4,4,64,256]{3,2,1,0:T(8,128)S(1)} fusion(f32[4,4]{1,0:T(4,128)S(1)} %copy-done.35, f32[4,4,256]{2,1,0:T(4,128)S(1)} %get-tuple-element.36, f32[4,4,256]{2,1,0:T(4,128)S(1)} %get-tuple-element.35, f32[4,4,256]{2,1,0:T(4,128)S(1)} %copy-done.18, f32[4,4,256]{2,1,0:T(4,128)S(1)} %copy-done.15, f32[64,4,4,256]{3,0,2,1:T(8,128)S(1)} %copy-done.5, ...), kind=kOutput, calls=%fused_computation.22 | convolution fusion | flops 820314112 | bytes 2424896 | tf_op jit(solution)/shard_map/xyij,mxyj->mxyi/dot_general | solution.py:53
  68.3 6.7 %fusion.175 = f32[64,4,4,256]{3,0,2,1:T(8,128)S(1)} fusion(f32[4,4]{1,0:T(4,128)S(1)} %copy-done.34, f32[4,4,256]{2,1,0:T(4,128)S(1)} %get-tuple-element.25, f32[4,4,256]{2,1,0:T(4,128)S(1)} %get-tuple-element.26, f32[4,4,256]{2,1,0:T(4,128)S(1)} %copy-done.18, f32[4,4,256]{2,1,0:T(4,128)S(1)} %copy-done.15, f32[64,6,5,256]{3,0,2,1:T(8,128)S(1)} %pad_maximum_fusion.57), kind=kOutput, calls=%fused_computation.191 | convolution fusion | flops 821035008 | bytes 3080256 | tf_op jit(solution)/shard_map/xyij,mxyj->mxyi/dot_general | solution.py:53
  75.7 6.9 %fusion.176 = f32[64,4,4,256]{3,0,2,1:T(8,128)S(1)} fusion(f32[4,4]{1,0:T(4,128)S(1)} %copy-done.33, f32[4,4,256]{2,1,0:T(4,128)S(1)} %get-tuple-element.31, f32[4,4,256]{2,1,0:T(4,128)S(1)} %get-tuple-element.32, f32[4,4,256]{2,1,0:T(4,128)S(1)} %copy-done.18, f32[4,4,256]{2,1,0:T(4,128)S(1)} %copy-done.15, f32[64,6,5,256]{3,0,2,1:T(8,128)S(1)} %pad_maximum_fusion.58), kind=kOutput, calls=%fused_computation.192 | convolution fusion | flops 821035008 | bytes 3080256 | tf_op jit(solution)/shard_map/xyij,mxyj->mxyi/dot_general | solution.py:53
  83.2 6.6 %fusion.6 = f32[4,4,64,256]{3,2,1,0:T(8,128)S(1)} fusion(f32[4,4]{1,0:T(4,128)S(1)} %copy-done.32, f32[4,4,256]{2,1,0:T(4,128)S(1)} %get-tuple-element.30, f32[4,4,256]{2,1,0:T(4,128)S(1)} %get-tuple-element.29, f32[4,4,256]{2,1,0:T(4,128)S(1)} %copy-done.18, f32[4,4,256]{2,1,0:T(4,128)S(1)} %copy-done.15, f32[64,6,5,256]{3,0,2,1:T(8,128)S(1)} %pad_maximum_fusion.52), kind=kOutput, calls=%fused_computation.18 | convolution fusion | flops 819986432 | bytes 3080256 | tf_op jit(solution)/shard_map/xyij,mxyj->mxyi/dot_general | solution.py:53
  90.5 7.1 %fusion.16 = f32[4,4,64,256]{3,2,1,0:T(8,128)S(1)} fusion(f32[4,4]{1,0:T(4,128)S(1)} %copy-done.31, f32[4,4,256]{2,1,0:T(4,128)S(1)} %get-tuple-element.23, f32[4,4,256]{2,1,0:T(4,128)S(1)} %get-tuple-element.22, f32[4,4,256]{2,1,0:T(4,128)S(1)} %copy-done.18, f32[4,4,256]{2,1,0:T(4,128)S(1)} %copy-done.15, f32[64,6,5,256]{3,0,2,1:T(8,128)S(1)} %pad_maximum_fusion.54), kind=kOutput, calls=%fused_computation.28 | convolution fusion | flops 821035008 | bytes 3080256 | tf_op jit(solution)/shard_map/xyij,mxyj->mxyi/dot_general | solution.py:53
  98.8 6.7 %fusion.206 = f32[64,4,4,256]{3,0,2,1:T(8,128)S(1)} fusion(f32[64,4,4,256]{3,0,2,1:T(8,128)S(1)} %copy-done.41, f32[4,4,64,256]{3,2,1,0:T(8,128)S(1)} %fusion.6, f32[4,4,64,256]{3,2,1,0:T(8,128)S(1)} %fusion.16, f32[4,4,64,256]{3,2,1,0:T(8,128)S(1)} %fusion.10, f32[4,4]{1,0:T(4,128)S(1)} %copy-done.30, f32[4,4,256]{2,1,0:T(4,128)S(1)} %get-tuple-element.28, ...), kind=kOutput, calls=%fused_computation.222 | convolution fusion | flops 822083584 | bytes 7274560 | tf_op jit(solution)/shard_map/xyij,mxyj->mxyi/dot_general | solution.py:53
  106.2 6.8 %fusion.209 = f32[64,4,4,256]{3,0,2,1:T(8,128)S(1)} fusion(f32[64,4,4,256]{3,0,2,1:T(8,128)S(1)} %fusion.175, f32[64,4,4,256]{3,0,2,1:T(8,128)S(1)} %fusion.177, f32[64,4,4,256]{3,0,2,1:T(8,128)S(1)} %fusion.176, f32[64,4,4,256]{3,0,2,1:T(8,128)S(1)} %fusion.206, f32[4,4]{1,0:T(4,128)S(1)} %copy-done.29, f32[4,4,256]{2,1,0:T(4,128)S(1)} %get-tuple-element.24, ...), kind=kOutput, calls=%fused_computation.225 | convolution fusion | flops 821035008 | bytes 7274560 | tf_op jit(solution)/shard_map/xyij,mxyj->mxyi/dot_general | solution.py:53
  113.1 1.6 copy.28
  114.7 6.0 %fusion.210 = f32[192,64]{1,0:T(8,128)S(1)} fusion(f32[64,4,4,256]{3,0,2,1:T(8,128)S(1)} %fusion.209, f32[192,4,4,256]{3,2,1,0:T(4,128)} %constant_dynamic-update-slice_fusion.10), kind=kOutput, calls=%fused_computation.226 | convolution fusion | flops 603979776 | bytes 4243456 | tf_op jit(solution)/shard_map/dot_general | solution.py:68
  120.8 2.7 reshape.77
  123.5 64.8 %psum.28 = f32[192,64]{1,0:T(8,128)S(1)} all-reduce(f32[192,64]{1,0:T(8,128)S(1)} %fusion.210), channel_id=1, replica_groups=mesh['groups'=2,'sx'=4,'sy'=2,'sz'=2] {'sx','sy','sz'}, use_global_device_ids=true, to_apply=%region_0.0 | all-reduce | flops 12288 | bytes 98304 | tf_op jit(solution)/shard_map/psum | solution.py:96
  188.3 3.3 convolution_subtract_fusion.1
  191.6 1.0 copy-done.1
  192.6 1.0 fusion.348
  193.6 57.9 %psum.29 = f32[64,64]{0,1:T(8,128)S(1)} all-reduce(f32[64,64]{0,1:T(8,128)S(1)} %fusion.348), channel_id=1, replica_groups=mesh['groups'=2,'sx'=4,'sy'=2,'sz'=2] {'sx','sy','sz'}, use_global_device_ids=true, to_apply=%region_1.0 | all-reduce | flops 4096 | bytes 32768 | tf_op jit(solution)/shard_map/psum | solution.py:98
  251.6 5.8 %cholesky.44 = f32[64,64]{1,0:T(8,128)S(1)} custom-call(f32[64,64]{1,0:T(8,128)S(1)} %fusion.224), custom_call_target="Cholesky" | custom-call | tf_op jit(solution)/shard_map/jit(cholesky)/cholesky | solution.py:99
  258.8 4.9 custom-call.6
  263.7 3.3 fusion.222
  266.9 2.9 reshape.79
  269.9 1.9 copy.31
  271.8 1.3 collective-permute-start.8
  273.2 1.3 collective-permute-start.9
  274.5 8.2 %fusion.3 = f32[4,4,64,256]{3,2,1,0:T(8,128)S(1)} fusion(f32[4,4]{1,0:T(4,128)S(1)} %copy-done.40, f32[4,4,256]{2,1,0:T(4,128)S(1)} %copy-done.19, f32[4,4,256]{2,1,0:T(4,128)S(1)} %copy-done.16, f32[64,4,4,256]{3,2,1,0:T(4,128)S(1)} %copy-done.3), kind=kOutput, calls=%fused_computation.15 | convolution fusion | flops 818937856 | bytes 2129984 | tf_op jit(solution)/shard_map/xyij,mxyj->mxyi/dot_general | solution.py:53
  283.5 1.3 collective-permute-start.11
  284.9 3.1 collective-permute-start.10
  288.0 7.2 %fusion.11 = f32[4,4,64,256]{3,2,1,0:T(8,128)S(1)} fusion(f32[4,4]{1,0:T(4,128)S(1)} %copy-done.38, f32[4,4,256]{2,1,0:T(4,128)S(1)} %copy-done.23, f32[4,4,256]{2,1,0:T(4,128)S(1)} %copy-done.21, f32[4,4,256]{2,1,0:T(4,128)S(1)} %copy-done.19, f32[4,4,256]{2,1,0:T(4,128)S(1)} %copy-done.16, f32[64,1,4,256]{3,0,2,1:T(8,128)S(1)} %collective-permute-done.9, ...), kind=kOutput, calls=%fused_computation.23 | convolution fusion | flops 820314112 | bytes 2424896 | tf_op jit(solution)/shard_map/xyij,mxyj->mxyi/dot_general | solution.py:53
  295.2 7.6 %fusion.9 = f32[4,4,64,256]{3,2,1,0:T(8,128)S(1)} fusion(f32[4,4]{1,0:T(4,128)S(1)} %copy-done.36, f32[4,4,256]{2,1,0:T(4,128)S(1)} %copy-done.27, f32[4,4,256]{2,1,0:T(4,128)S(1)} %copy-done.25, f32[4,4,256]{2,1,0:T(4,128)S(1)} %copy-done.19, f32[4,4,256]{2,1,0:T(4,128)S(1)} %copy-done.16, f32[64,4,4,256]{3,0,2,1:T(8,128)S(1)} %copy.31, ...), kind=kOutput, calls=%fused_computation.21 | convolution fusion | flops 820314112 | bytes 2424896 | tf_op jit(solution)/shard_map/xyij,mxyj->mxyi/dot_general | solution.py:53
  303.6 6.7 %fusion.19 = f32[4,4,64,256]{3,2,1,0:T(8,128)S(1)} fusion(f32[4,4]{1,0:T(4,128)S(1)} %copy-done.34, f32[4,4,256]{2,1,0:T(4,128)S(1)} %get-tuple-element.25, f32[4,4,256]{2,1,0:T(4,128)S(1)} %copy-done.9, f32[4,4,256]{2,1,0:T(4,128)S(1)} %copy-done.19, f32[4,4,256]{2,1,0:T(4,128)S(1)} %copy-done.16, f32[64,6,5,256]{3,0,2,1:T(8,128)S(1)} %pad_maximum_fusion.56), kind=kOutput, calls=%fused_computation.31 | convolution fusion | flops 821035008 | bytes 3080256 | tf_op jit(solution)/shard_map/xyij,mxyj->mxyi/dot_general | solution.py:53
  311.0 6.8 %fusion.17 = f32[4,4,64,256]{3,2,1,0:T(8,128)S(1)} fusion(f32[4,4]{1,0:T(4,128)S(1)} %copy-done.33, f32[4,4,256]{2,1,0:T(4,128)S(1)} %copy-done.11, f32[4,4,256]{2,1,0:T(4,128)S(1)} %copy-done.13, f32[4,4,256]{2,1,0:T(4,128)S(1)} %copy-done.19, f32[4,4,256]{2,1,0:T(4,128)S(1)} %copy-done.16, f32[64,6,5,256]{3,0,2,1:T(8,128)S(1)} %pad_maximum_fusion.55), kind=kOutput, calls=%fused_computation.29 | convolution fusion | flops 821035008 | bytes 3080256 | tf_op jit(solution)/shard_map/xyij,mxyj->mxyi/dot_general | solution.py:53
  318.0 6.6 %fusion.5 = f32[4,4,64,256]{3,2,1,0:T(8,128)S(1)} fusion(f32[4,4]{1,0:T(4,128)S(1)} %copy-done.32, f32[4,4,256]{2,1,0:T(4,128)S(1)} %get-tuple-element.30, f32[4,4,256]{2,1,0:T(4,128)S(1)} %get-tuple-element.29, f32[4,4,256]{2,1,0:T(4,128)S(1)} %copy-done.19, f32[4,4,256]{2,1,0:T(4,128)S(1)} %copy-done.16, f32[64,6,5,256]{3,0,2,1:T(8,128)S(1)} %pad_maximum_fusion.51), kind=kOutput, calls=%fused_computation.17 | convolution fusion | flops 819986432 | bytes 3080256 | tf_op jit(solution)/shard_map/xyij,mxyj->mxyi/dot_general | solution.py:53
  324.9 6.9 %fusion.15 = f32[4,4,64,256]{3,2,1,0:T(8,128)S(1)} fusion(f32[4,4]{1,0:T(4,128)S(1)} %copy-done.31, f32[4,4,256]{2,1,0:T(4,128)S(1)} %get-tuple-element.23, f32[4,4,256]{2,1,0:T(4,128)S(1)} %get-tuple-element.22, f32[4,4,256]{2,1,0:T(4,128)S(1)} %copy-done.19, f32[4,4,256]{2,1,0:T(4,128)S(1)} %copy-done.16, f32[64,6,5,256]{3,0,2,1:T(8,128)S(1)} %pad_maximum_fusion.53), kind=kOutput, calls=%fused_computation.27 | convolution fusion | flops 821035008 | bytes 3080256 | tf_op jit(solution)/shard_map/xyij,mxyj->mxyi/dot_general | solution.py:53
  331.9 6.7 %fusion.202 = f32[4,4,64,256]{3,2,1,0:T(8,128)S(1)} fusion(f32[4,4,64,256]{3,2,1,0:T(8,128)S(1)} %fusion.3, f32[4,4,64,256]{3,2,1,0:T(8,128)S(1)} %fusion.5, f32[4,4,64,256]{3,2,1,0:T(8,128)S(1)} %fusion.15, f32[4,4,64,256]{3,2,1,0:T(8,128)S(1)} %fusion.9, f32[4,4]{1,0:T(4,128)S(1)} %copy-done.30, f32[4,4,256]{2,1,0:T(4,128)S(1)} %get-tuple-element.28, ...), kind=kOutput, calls=%fused_computation.218 | convolution fusion | flops 822083584 | bytes 7274560 | tf_op jit(solution)/shard_map/xyij,mxyj->mxyi/dot_general | solution.py:53
  338.9 7.1 %fusion.199 = f32[64,4,4,256]{3,0,2,1:T(8,128)S(1)} fusion(f32[4,4,64,256]{3,2,1,0:T(8,128)S(1)} %fusion.19, f32[4,4,64,256]{3,2,1,0:T(8,128)S(1)} %fusion.11, f32[4,4,64,256]{3,2,1,0:T(8,128)S(1)} %fusion.17, f32[4,4,64,256]{3,2,1,0:T(8,128)S(1)} %fusion.202, f32[4,4]{1,0:T(4,128)S(1)} %copy-done.29, f32[4,4,256]{2,1,0:T(4,128)S(1)} %get-tuple-element.24, ...), kind=kOutput, calls=%fused_computation.215 | convolution fusion | flops 821035008 | bytes 7274560 | tf_op jit(solution)/shard_map/xyij,mxyj->mxyi/dot_general | solution.py:53
  345.9 1.6 copy.37
  347.6 2.7 reshape.80
  350.3 5.6 %fusion = f32[256,64]{1,0:T(8,128)} fusion(f32[64,4096]{1,0:T(8,128)} %reshape.80, f32[64,4096]{1,0:T(8,128)} %fusion.222, f32[192,4096]{1,0:T(8,128)S(1)} %reshape.78), kind=kOutput, calls=%fused_computation.12 | convolution fusion | flops 806354944 | bytes 5308416 | tf_op jit(solution)/shard_map/dot_general | solution.py:68
  355.9 86.5 %all-reduce.2.cloned.1.call-done = f32[256,64]{1,0:T(8,128)} async-done(((f32[256,64]{1,0:T(8,128)}), f32[256,64]{1,0:T(8,128)}) %all-reduce.2.cloned.1.call-update) | async-done | bytes 65552 | tf_op jit(solution)/shard_map/psum | solution.py:96
  442.4 4.3 convolution_subtract_fusion
  446.7 1.0 copy-done
  447.7 1.0 fusion.349
  448.7 60.0 %psum.31 = f32[64,64]{0,1:T(8,128)S(1)} all-reduce(f32[64,64]{0,1:T(8,128)S(1)} %fusion.349), channel_id=1, replica_groups=mesh['groups'=2,'sx'=4,'sy'=2,'sz'=2] {'sx','sy','sz'}, use_global_device_ids=true, to_apply=%region_5.8 | all-reduce | flops 4096 | bytes 32768 | tf_op jit(solution)/shard_map/psum | solution.py:98
  508.8 5.8 %cholesky.55 = f32[64,64]{1,0:T(8,128)S(1)} custom-call(f32[64,64]{1,0:T(8,128)S(1)} %fusion.221), custom_call_target="Cholesky" | custom-call | tf_op jit(solution)/shard_map/jit(cholesky)/cholesky | solution.py:99
  515.9 4.9 custom-call.7
  520.8 2.3 fusion.219
  523.1 1.7 reshape.81
  (137 shorter events, 11.3 us)
Async XLA Ops:
  7.2 15.8 %copy-start.7 = (f32[2,4,4,256]{3,2,1,0:T(4,128)S(1)}, f32[2,4,4,256]{3,2,1,0:T(4,128)}, u32[]{:S(2)}) copy-start(f32[2,4,4,256]{3,2,1,0:T(4,128)} %param.9) | copy-start | bytes 98308
  7.2 15.8 %copy-start.28 = (s32[9,4,4]{0,2,1:T(4,128)S(1)}, s32[9,4,4]{0,2,1:T(4,128)}, u32[]{:S(2)}) copy-start(s32[9,4,4]{0,2,1:T(4,128)} %param.10) | copy-start | bytes 1732
  7.2 435.2 %all-reduce.2.cloned.1.call-start = ((), (), s32[]{:S(2)}) async-start(), calls=%async_computation | async-start | bytes 262144 | tf_op jit(solution)/shard_map/psum | solution.py:96
  7.2 16.6 %copy-start.6 = (f32[128,4,4,256]{3,2,1,0:T(4,128)S(1)}, f32[128,4,4,256]{3,2,1,0:T(4,128)}, u32[]{:S(2)}) copy-start(f32[128,4,4,256]{3,2,1,0:T(4,128)} %param.7) | copy-start | bytes 6291460
  8.1 30.6 %collective-permute-start.3 = (f32[2,1,4,256]{3,2,1,0:T(4,128)S(1)}, f32[2,1,4,256]{3,2,1,0:T(4,128)S(1)}, u32[]{:S(2)}, u32[]{:S(2)}) collective-permute-start(f32[2,1,4,256]{3,2,1,0:T(4,128)S(1)} %get-tuple-element.45), channel_id=1, source_target_pairs={{0,4},{4,8},{8,12},{1,5},{5,9},{9,13},{2,6},{6,10},{10,14},{3,7},{... | collective-permute-start | bytes 24584 | tf_op jit(solution)/shard_map/ppermute | solution.py:14
  13.0 25.8 %collective-permute-start.4 = (f32[2,1,4,256]{3,2,1,0:T(4,128)S(1)}, f32[2,1,4,256]{3,2,1,0:T(4,128)S(1)}, u32[]{:S(2)}, u32[]{:S(2)}) collective-permute-start(f32[2,1,4,256]{3,2,1,0:T(4,128)S(1)} %get-tuple-element.44), channel_id=1, source_target_pairs={{4,0},{8,4},{12,8},{5,1},{9,5},{13,9},{6,2},{10,6},{14,10},{7,3},{... | collective-permute-start | bytes 24584 | tf_op jit(solution)/shard_map/ppermute | solution.py:17
  16.2 17.8 %copy-start.4 = (f32[64,4,4,256]{3,0,2,1:T(8,128)}, f32[64,4,4,256]{3,0,2,1:T(8,128)S(1)}, u32[]{:S(2)}) copy-start(f32[64,4,4,256]{3,0,2,1:T(8,128)S(1)} %copy.22) | copy-start | bytes 3145732
  16.2 9.4 %copy-start.2 = (f32[64,4,4,256]{3,2,1,0:T(4,128)S(1)}, f32[64,4,4,256]{3,2,1,0:T(4,128)}, u32[]{:S(2)}) copy-start(f32[64,4,4,256]{3,2,1,0:T(4,128)} %param.8) | copy-start | bytes 3145732
  17.0 27.2 %collective-permute-start = (f32[64,1,4,256]{3,0,2,1:T(8,128)}, f32[64,1,4,256]{3,0,2,1:T(8,128)S(1)}, u32[]{:S(2)}, u32[]{:S(2)}) collective-permute-start(f32[64,1,4,256]{3,0,2,1:T(8,128)} %get-tuple-element.20), channel_id=1, source_target_pairs={{0,4},{4,8},{8,12},{1,5},{5,9},{9,13},{2,6},{6,10},{10,14},{3,7},{... | collective-permute-start | bytes 786440 | tf_op jit(solution)/shard_map/ppermute | solution.py:14
  21.7 24.4 %collective-permute-start.1 = (f32[64,1,4,256]{3,0,2,1:T(8,128)}, f32[64,1,4,256]{3,0,2,1:T(8,128)}, u32[]{:S(2)}, u32[]{:S(2)}) collective-permute-start(f32[64,1,4,256]{3,0,2,1:T(8,128)} %get-tuple-element.19), channel_id=1, source_target_pairs={{4,0},{8,4},{12,8},{5,1},{9,5},{13,9},{6,2},{10,6},{14,10},{7,3},{... | collective-permute-start | bytes 786440 | tf_op jit(solution)/shard_map/ppermute | solution.py:17
  23.0 10.9 %copy-start.14 = (f32[4,4,256]{2,1,0:T(4,128)}, f32[4,4,256]{2,1,0:T(4,128)S(1)}, u32[]{:S(2)}) copy-start(f32[4,4,256]{2,1,0:T(4,128)S(1)} %get-tuple-element.42) | copy-start | bytes 49156
  23.0 10.9 %copy-start.17 = (f32[4,4,256]{2,1,0:T(4,128)}, f32[4,4,256]{2,1,0:T(4,128)S(1)}, u32[]{:S(2)}) copy-start(f32[4,4,256]{2,1,0:T(4,128)S(1)} %get-tuple-element.43) | copy-start | bytes 49156
  23.9 10.1 %copy-start.39 = (f32[4,4]{1,0:T(4,128)}, f32[4,4]{1,0:T(4,128)S(1)}, u32[]{:S(2)}) copy-start(f32[4,4]{1,0:T(4,128)S(1)} %get-tuple-element.8) | copy-start | bytes 196
  38.7 13.4 %copy-start.5 = (f32[64,4,4,256]{3,0,2,1:T(8,128)S(1)}, f32[64,4,4,256]{3,0,2,1:T(8,128)}, u32[]{:S(2)}) copy-start(f32[64,4,4,256]{3,0,2,1:T(8,128)} %copy-done.4) | copy-start | bytes 3145732
  38.7 13.4 %copy-start.15 = (f32[4,4,256]{2,1,0:T(4,128)S(1)}, f32[4,4,256]{2,1,0:T(4,128)}, u32[]{:S(2)}) copy-start(f32[4,4,256]{2,1,0:T(4,128)} %copy-done.14) | copy-start | bytes 49156
  38.7 13.4 %copy-start.18 = (f32[4,4,256]{2,1,0:T(4,128)S(1)}, f32[4,4,256]{2,1,0:T(4,128)}, u32[]{:S(2)}) copy-start(f32[4,4,256]{2,1,0:T(4,128)} %copy-done.17) | copy-start | bytes 49156
  38.7 13.4 %copy-start.37 = (f32[4,4]{1,0:T(4,128)S(1)}, f32[4,4]{1,0:T(4,128)}, u32[]{:S(2)}) copy-start(f32[4,4]{1,0:T(4,128)} %get-tuple-element.6) | copy-start | bytes 196
  38.8 4.5 collective-permute-start.7
  40.3 20.0 %copy-start.20 = (f32[4,4,256]{2,1,0:T(4,128)}, f32[4,4,256]{2,1,0:T(4,128)S(1)}, u32[]{:S(2)}) copy-start(f32[4,4,256]{2,1,0:T(4,128)S(1)} %get-tuple-element.37) | copy-start | bytes 49156
  40.3 20.0 %copy-start.22 = (f32[4,4,256]{2,1,0:T(4,128)}, f32[4,4,256]{2,1,0:T(4,128)S(1)}, u32[]{:S(2)}) copy-start(f32[4,4,256]{2,1,0:T(4,128)S(1)} %get-tuple-element.38) | copy-start | bytes 49156
  40.3 3.9 collective-permute-start.5
  43.4 16.9 %copy-start.24 = (f32[4,4,256]{2,1,0:T(4,128)}, f32[4,4,256]{2,1,0:T(4,128)S(1)}, u32[]{:S(2)}) copy-start(f32[4,4,256]{2,1,0:T(4,128)S(1)} %get-tuple-element.35) | copy-start | bytes 49156
  43.4 16.9 %copy-start.26 = (f32[4,4,256]{2,1,0:T(4,128)}, f32[4,4,256]{2,1,0:T(4,128)S(1)}, u32[]{:S(2)}) copy-start(f32[4,4,256]{2,1,0:T(4,128)S(1)} %get-tuple-element.36) | copy-start | bytes 49156
  43.4 24.5 %copy-start.8 = (f32[4,4,256]{2,1,0:T(4,128)}, f32[4,4,256]{2,1,0:T(4,128)S(1)}, u32[]{:S(2)}) copy-start(f32[4,4,256]{2,1,0:T(4,128)S(1)} %get-tuple-element.26) | copy-start | bytes 49156
  44.2 31.0 %copy-start.10 = (f32[4,4,256]{2,1,0:T(4,128)}, f32[4,4,256]{2,1,0:T(4,128)S(1)}, u32[]{:S(2)}) copy-start(f32[4,4,256]{2,1,0:T(4,128)S(1)} %get-tuple-element.31) | copy-start | bytes 49156
  44.2 31.0 %copy-start.12 = (f32[4,4,256]{2,1,0:T(4,128)}, f32[4,4,256]{2,1,0:T(4,128)S(1)}, u32[]{:S(2)}) copy-start(f32[4,4,256]{2,1,0:T(4,128)S(1)} %get-tuple-element.32) | copy-start | bytes 49156
  47.1 20.6 %collective-permute-start.6 = (f32[64,6,1,256]{3,0,2,1:T(8,128)S(1)}, f32[64,6,1,256]{3,0,2,1:T(8,128)S(1)}, u32[]{:S(2)}, u32[]{:S(2)}) collective-permute-start(f32[64,6,1,256]{3,0,2,1:T(8,128)S(1)} %get-tuple-element.16), channel_id=1, source_target_pairs={{1,0},{2,1},{3,2},{5,4},{6,5},{7,6},{9,8},{10,9},{11,10},{13,12},{... | collective-permute-start | bytes 1179656 | tf_op jit(solution)/shard_map/ppermute | solution.py:17
  48.4 26.6 %collective-permute-start.2 = (f32[64,6,1,256]{3,0,2,1:T(8,128)S(1)}, f32[64,6,1,256]{3,0,2,1:T(8,128)S(1)}, u32[]{:S(2)}, u32[]{:S(2)}) collective-permute-start(f32[64,6,1,256]{3,0,2,1:T(8,128)S(1)} %get-tuple-element.15), channel_id=1, source_target_pairs={{0,1},{1,2},{2,3},{4,5},{5,6},{6,7},{8,9},{9,10},{10,11},{12,13},{... | collective-permute-start | bytes 1179656 | tf_op jit(solution)/shard_map/ppermute | solution.py:14
  52.1 8.1 %copy-start.35 = (f32[4,4]{1,0:T(4,128)S(1)}, f32[4,4]{1,0:T(4,128)}, u32[]{:S(2)}) copy-start(f32[4,4]{1,0:T(4,128)} %get-tuple-element.11) | copy-start | bytes 196
  67.7 0.7 copy-start.34
  75.0 0.7 copy-start.33
  82.6 0.7 copy-start.32
  89.9 0.7 copy-start.31
  97.6 0.7 copy-start.30
  97.6 1.2 copy-start.41
  105.6 0.7 copy-start.29
  191.6 1.0 copy-start.1
  266.9 7.5 %copy-start.16 = (f32[4,4,256]{2,1,0:T(4,128)S(1)}, f32[4,4,256]{2,1,0:T(4,128)}, u32[]{:S(2)}) copy-start(f32[4,4,256]{2,1,0:T(4,128)} %copy-done.14) | copy-start | bytes 49156
  266.9 7.5 %copy-start.19 = (f32[4,4,256]{2,1,0:T(4,128)S(1)}, f32[4,4,256]{2,1,0:T(4,128)}, u32[]{:S(2)}) copy-start(f32[4,4,256]{2,1,0:T(4,128)} %copy-done.17) | copy-start | bytes 49156
  266.9 7.5 %copy-start.40 = (f32[4,4]{1,0:T(4,128)S(1)}, f32[4,4]{1,0:T(4,128)}, u32[]{:S(2)}) copy-start(f32[4,4]{1,0:T(4,128)} %copy-done.39) | copy-start | bytes 196
  269.9 4.6 copy-start.3
  271.8 10.9 %collective-permute-start.8 = (f32[64,1,4,256]{3,0,2,1:T(8,128)S(1)}, f32[64,1,4,256]{3,0,2,1:T(8,128)S(1)}, u32[]{:S(2)}, u32[]{:S(2)}) collective-permute-start(f32[64,1,4,256]{3,0,2,1:T(8,128)S(1)} %get-tuple-element.18), channel_id=1, source_target_pairs={{0,4},{4,8},{8,12},{1,5},{5,9},{9,13},{2,6},{6,10},{10,14},{3,7},{... | collective-permute-start | bytes 786440 | tf_op jit(solution)/shard_map/ppermute | solution.py:14
  273.2 10.3 %collective-permute-start.9 = (f32[64,1,4,256]{3,0,2,1:T(8,128)S(1)}, f32[64,1,4,256]{3,0,2,1:T(8,128)S(1)}, u32[]{:S(2)}, u32[]{:S(2)}) collective-permute-start(f32[64,1,4,256]{3,0,2,1:T(8,128)S(1)} %get-tuple-element.17), channel_id=1, source_target_pairs={{4,0},{8,4},{12,8},{5,1},{9,5},{13,9},{6,2},{10,6},{14,10},{7,3},{... | collective-permute-start | bytes 786440 | tf_op jit(solution)/shard_map/ppermute | solution.py:17
  282.8 5.2 copy-start.21
  282.8 5.2 copy-start.23
  282.8 5.2 copy-start.38
  283.5 19.3 %collective-permute-start.11 = (f32[64,6,1,256]{3,0,2,1:T(8,128)S(1)}, f32[64,6,1,256]{3,0,2,1:T(8,128)S(1)}, u32[]{:S(2)}, u32[]{:S(2)}) collective-permute-start(f32[64,6,1,256]{3,0,2,1:T(8,128)S(1)} %get-tuple-element.14), channel_id=1, source_target_pairs={{1,0},{2,1},{3,2},{5,4},{6,5},{7,6},{9,8},{10,9},{11,10},{13,12},{... | collective-permute-start | bytes 1179656 | tf_op jit(solution)/shard_map/ppermute | solution.py:17
  284.8 10.4 %copy-start.25 = (f32[4,4,256]{2,1,0:T(4,128)S(1)}, f32[4,4,256]{2,1,0:T(4,128)}, u32[]{:S(2)}) copy-start(f32[4,4,256]{2,1,0:T(4,128)} %copy-done.24) | copy-start | bytes 49156
  284.8 10.4 %copy-start.27 = (f32[4,4,256]{2,1,0:T(4,128)S(1)}, f32[4,4,256]{2,1,0:T(4,128)}, u32[]{:S(2)}) copy-start(f32[4,4,256]{2,1,0:T(4,128)} %copy-done.26) | copy-start | bytes 49156
  284.9 10.4 %copy-start.36 = (f32[4,4]{1,0:T(4,128)S(1)}, f32[4,4]{1,0:T(4,128)}, u32[]{:S(2)}) copy-start(f32[4,4]{1,0:T(4,128)} %get-tuple-element.11) | copy-start | bytes 196
  284.9 25.4 %collective-permute-start.10 = (f32[64,6,1,256]{3,0,2,1:T(8,128)S(1)}, f32[64,6,1,256]{3,0,2,1:T(8,128)S(1)}, u32[]{:S(2)}, u32[]{:S(2)}) collective-permute-start(f32[64,6,1,256]{3,0,2,1:T(8,128)S(1)} %get-tuple-element.13), channel_id=1, source_target_pairs={{0,1},{1,2},{2,3},{4,5},{5,6},{6,7},{8,9},{9,10},{10,11},{12,13},{... | collective-permute-start | bytes 1179656 | tf_op jit(solution)/shard_map/ppermute | solution.py:14
  302.9 0.7 copy-start.9
  310.3 0.7 copy-start.11
  310.3 0.7 copy-start.13
  446.7 1.0 copy-start
Sparse Core Ops, SparseCore 0:
  356.1 86.3 all-reduce.1
where the time goes:
time: 540 us; the launch traced here: 532 us
  blocking collectives  183 us (34%)
  matrix products  155 us (29%)
  waiting for transfers between devices  87.3 us (16%)
  local copies, waits for them, and re-layouts  35.5 us (7%)
  starting transfers between devices  28.6 us (5%)
  other arithmetic  27.3 us (5%)
  between operations  15.3 us (3%)
    dot_general x18, matrix products, coupling(): jnp.einsum('xyij,mxyj->mxyi', weights[code], near, precision=lax.Precisio...  128 us
    psum x2, blocking collectives, lanczos_step(): lax.psum(inner(flat_image, flat_image), ('sx', 'sy', 'sz')) / sites_total  118 us
    psum x1, waiting for transfers between devices, lanczos_step(): lax.psum(inner(flat_span, flat_image), ('sx', 'sy', 'sz')) / sites_total  86.5 us
    psum x1, blocking collectives, lanczos_step(): lax.psum(inner(flat_span, flat_image), ('sx', 'sy', 'sz')) / sites_total  64.8 us
    ppermute x6, starting transfers between devices, extended(): lax.ppermute(lax.slice_in_dim(block, block.shape[dim] - width, None, axis...  20.6 us
    dot_general x4, matrix products, inner(): lax.dot_general(left, right, (((1,), (1,)), ((), ())), precision=lax.Prec...  13.6 us
    another operation x6, other arithmetic, lanczos_step(): lower = jnp.linalg.cholesky(gram)  13.1 us
    unnamed x91, local copies, waits for them, and re-layouts  12.5 us
  transfers between devices with their start and end apart: 13, of which 2 were waited for; matrix products, arithmetic and copies ran while one was open for 14% of the time, Pallas kernels for 0%

commit v1 on v0

v1 whole, which is shorter than its diff:
```python
import functools

import jax
import jax.numpy as jnp
from jax import lax
from jax.experimental import pallas as pl
from jax.experimental.pallas import tpu as pltpu
from jax.sharding import PartitionSpec as P

GAIN = 0.0625
MESH = pl.DeviceIdType.MESH
F32 = jnp.float32
BF16 = jnp.bfloat16
HIGH = lax.Precision.HIGHEST
DIRS = [(da, db) for da in (-1, 0, 1) for db in (-1, 0, 1) if (da, db) != (0, 0)]


def dot_nn(left, right):
    return lax.dot_general(
        left, right, (((1,), (0,)), ((), ())), precision=HIGH, preferred_element_type=F32
    )


def dot_nt(left, right):
    return lax.dot_general(
        left, right, (((1,), (1,)), ((), ())), precision=HIGH, preferred_element_type=F32
    )


def dot_fast(left, right):
    return lax.dot_general(
        left, right, (((1,), (0,)), ((), ())), preferred_element_type=F32
    )


def inverse_factor(gram):
    size = gram.shape[0]
    rows = lax.broadcasted_iota(jnp.int32, (size, size), 0)
    cols = lax.broadcasted_iota(jnp.int32, (size, size), 1)
    eye = jnp.where(rows == cols, 1.0, 0.0).astype(F32)
    work = jnp.concatenate([eye, gram], axis=1)
    wide = 2 * size
    rowid = lax.broadcasted_iota(jnp.int32, (size, wide), 0)
    pivots = jnp.ones((size, wide), F32)
    panel = 8
    for base in range(0, size, panel):
        cast = [
            jnp.broadcast_to(work[:, size + base + c : size + base + c + 1], (size, wide))
            for c in range(panel)
        ]
        for c in range(panel):
            k = base + c
            pivot = cast[c][k : k + 1, :]
            pivots = jnp.where(rowid == k, pivot, pivots)
            factor = jnp.where(rowid > k, cast[c] * (1.0 / pivot), 0.0)
            work = work - factor * work[k : k + 1, :]
            for d in range(c + 1, panel):
                cast[d] = cast[d] - factor * cast[d][k : k + 1, :]
    scaled = work * lax.rsqrt(pivots)
    return scaled[:, :size]


def body(
    nsx, nsy, nsz, tx, ty,
    links, prior_in, cur_in, pos_in,
    first_out, second_out,
    khi, klo, span, vpad, vbf, ppad, ncol, grams, mix,
    ss_x, ss_a, ss_b, ss_z, ss_y,
    r1_x, r1_a, r1_b, r1_z, r1_y,
    r2_x, r2_a, r2_b, r2_z, r2_y,
    load_sem, pos_s, pos_r, v1_s, v1_r, v2_s, v2_r, pl_s, pl_r, z_s, z_r, g_s, g_r,
):
    nq = nsy * nsz
    group = lax.axis_index("groups")
    sx = lax.axis_index("sx")
    q = lax.axis_index("sy") * nsz + lax.axis_index("sz")
    prev = prior_in.shape[1]
    width = cur_in.shape[1]
    total_sites = float(tx * ty * 256 * nsx * nq)
    tiles = tx * ty

    def device(s, p):
        return (group, s, p // nsz, lax.rem(p, nsz))

    def exists(d):
        s, p = sx + d[0], q + d[1]
        return (s >= 0) & (s < nsx) & (p >= 0) & (p < nq)

    loads = []
    for a in range(tx):
        loads.append(pltpu.make_async_copy(
            cur_in.at[pl.ds(a * ty, ty)], vpad.at[a + 1, pl.ds(1, ty)], load_sem.at[a]))
        loads.append(pltpu.make_async_copy(
            pos_in.at[pl.ds(a * ty, ty)], ppad.at[a + 1, pl.ds(1, ty)], load_sem.at[tx + a]))
    prior_load = pltpu.make_async_copy(prior_in, span.at[:, pl.ds(0, prev)], load_sem.at[2 * tx])
    cur_load = pltpu.make_async_copy(
        cur_in, span.at[:, pl.ds(prev + width, width)], load_sem.at[2 * tx + 1])
    for a in range(tx + 2):
        for b in range(ty + 2):
            if a in (0, tx + 1) or b in (0, ty + 1):
                vpad[a, b] = jnp.zeros((width, 256), F32)
                ppad[a, b] = jnp.zeros((2, 256), F32)
    for load in loads:
        load.start()
    prior_load.start()
    cur_load.start()

    barrier = pltpu.get_barrier_semaphore()
    expected = jnp.int32(nq - 1 + nsx - 1)
    for d in DIRS:
        ok = exists(d)
        expected = expected + jnp.where(ok, 1, 0)

        @pl.when(ok)
        def _(d=d):
            pl.semaphore_signal(
                barrier, inc=1, device_id=device(sx + d[0], q + d[1]), device_id_type=MESH)
    for k in range(1, nq):
        pl.semaphore_signal(
            barrier, inc=1, device_id=device(sx, lax.rem(q + k, nq)), device_id_type=MESH)
    for k in range(1, nsx):
        pl.semaphore_signal(
            barrier, inc=1, device_id=device(lax.rem(sx + k, nsx), q), device_id_type=MESH)
    pl.semaphore_wait(barrier, expected)
    for load in loads:
        load.wait()

    def pick(shift, count):
        src = {-1: pl.ds(1, 1), 0: pl.ds(1, count), 1: pl.ds(count, 1)}[shift]
        dst = {-1: pl.ds(count + 1, 1), 0: pl.ds(1, count), 1: pl.ds(0, 1)}[shift]
        return src, dst

    def halo_copy(ref, i, send, recv):
        d = DIRS[i]
        (sa, da), (sb, db) = pick(d[0], tx), pick(d[1], ty)
        return pltpu.make_async_remote_copy(
            src_ref=ref.at[sa, sb], dst_ref=ref.at[da, db],
            send_sem=send.at[i], recv_sem=recv.at[i],
            device_id=device(sx + d[0], q + d[1]), device_id_type=MESH)

    def halo_start(ref, send, recv):
        for i, d in enumerate(DIRS):
            @pl.when(exists(d))
            def _(i=i):
                halo_copy(ref, i, send, recv).start()

    def halo_wait(ref, send, recv):
        for i, d in enumerate(DIRS):
            @pl.when(exists(d))
            def _(i=i):
                halo_copy(ref, i, send, recv).wait_send()

            @pl.when(exists((-d[0], -d[1])))
            def _(i=i):
                halo_copy(ref, i, send, recv).wait_recv()

    class Reduce:
        def __init__(self, which, x, a, b, z, y):
            self.w, self.x, self.a, self.b, self.z, self.y = which, x, a, b, z, y

        def plane(self, k):
            to = lax.rem(q + k, nq)
            return pltpu.make_async_remote_copy(
                src_ref=self.x.at[to], dst_ref=self.a.at[k - 1],
                send_sem=pl_s.at[self.w, k - 1], recv_sem=pl_r.at[self.w, k - 1],
                device_id=device(sx, to), device_id_type=MESH)

        def line(self, k):
            to = lax.rem(sx + k, nsx)
            return pltpu.make_async_remote_copy(
                src_ref=self.z, dst_ref=self.b.at[sx],
                send_sem=z_s.at[self.w, k - 1], recv_sem=z_r.at[self.w, k - 1],
                device_id=device(to, q), device_id_type=MESH)

        def back(self, k):
            to = lax.rem(q + k, nq)
            return pltpu.make_async_remote_copy(
                src_ref=self.y.at[q], dst_ref=self.y.at[q],
                send_sem=g_s.at[self.w, k - 1], recv_sem=g_r.at[self.w, k - 1],
                device_id=device(sx, to), device_id_type=MESH)

        def start(self):
            for k in range(1, nq):
                self.plane(k).start()

        def second(self):
            for k in range(1, nq):
                self.plane(k).wait()
            part = self.x[q]
            for k in range(1, nq):
                part = part + self.a[k - 1]
            self.z[...] = part
            for k in range(1, nsx):
                self.line(k).start()
            self.b[sx] = part

        def third(self):
            for k in range(1, nsx):
                self.line(k).wait()
            part = self.b[0]
            for k in range(1, nsx):
                part = part + self.b[k]
            self.y[q] = part * (1.0 / total_sites)
            for k in range(1, nq):
                self.back(k).start()

        def finish(self):
            for k in range(1, nq):
                self.back(k).wait()

    reduce_ss = Reduce(0, ss_x, ss_a, ss_b, ss_z, ss_y)
    reduce_1 = Reduce(1, r1_x, r1_a, r1_b, r1_z, r1_y)
    reduce_2 = Reduce(2, r2_x, r2_a, r2_b, r2_z, r2_y)

    halo_start(ppad, pos_s, pos_r)
    halo_start(vpad, v1_s, v1_r)

    def split(a, b):
        value = vpad[a, b]
        high = value.astype(BF16)
        vbf[a, b, 0:width] = high
        vbf[a, b, width : 2 * width] = (value - high.astype(F32)).astype(BF16)

    def interior(a, b):
        return (a >= 1) & (a <= tx) & (b >= 1) & (b <= ty)

    def make_block(na, nb, code):
        da, db = code // 3 - 1, code % 3 - 1
        oa, ob = na - da, nb - db
        own = (oa - 1) * ty + (ob - 1)

        @pl.when(interior(oa, ob))
        def _():
            link = links[code * tiles + own].astype(F32) * GAIN
            c1 = link
            c4 = link * 4.0
            place = own * 9 + code
            xrow = ppad[oa, ob, 0:1, :] - float(da)
            yrow = ppad[oa, ob, 1:2, :] - float(db)
            step = 32
            for j in range(0, 256, step):
                nx = ncol[0, j : j + step, :]
                ny = ncol[1, j : j + step, :]
                for half in range(0, 256, 128):
                    dx = nx - xrow[:, half : half + 128]
                    dy = ny - yrow[:, half : half + 128]
                    sq = dx * dx + dy * dy
                    dist = sq * lax.rsqrt(jnp.maximum(sq, 1e-30))
                    fall = jnp.maximum(1.0 - dist, 0.0)
                    two = fall * fall
                    value = (two * two) * (dist * c4 + c1)
                    high = value.astype(BF16)
                    khi[place, j : j + step, half : half + 128] = high
                    klo[place, j : j + step, half : half + 128] = (
                        value - high.astype(F32)).astype(BF16)
            apply_block(na, nb, place, own, prev)

    def apply_block(na, nb, place, own, base):
        both = dot_fast(vbf[na, nb], khi[place])
        low = dot_fast(vbf[na, nb, 0:width], klo[place])
        rows = pl.ds(base, width)
        span[own, rows] = span[own, rows] + (both[0:width] + both[width : 2 * width] + low)

    def make_near(na, nb):
        split(na, nb)
        for c in range(2):
            row = ppad[na, nb, c : c + 1, :]
            ncol[c] = jnp.transpose(jnp.broadcast_to(row, (128, 256)))
        for code in range(9):
            make_block(na, nb, code)

    def clear(t, base):
        span[t, pl.ds(base, width)] = jnp.zeros((width, 256), F32)

    @pl.loop(0, tiles)
    def _(t):
        clear(t, prev)
        clear(t, prev + 2 * width)

    prior_load.wait()
    cur_load.wait()
    full = prev + 2 * width
    for part in range(2):
        grams[...] = jnp.zeros_like(grams)
        rows = pl.ds(0, prev) if part == 0 else pl.ds(prev + width, width)
        size = prev if part == 0 else width

        @pl.loop(0, tiles)
        def _(t):
            grams[0:size, :] = grams[0:size, :] + dot_nt(span[t, rows], span[t, 0:full])
        chunk = ss_x.shape[1]
        offset = 0 if part == 0 else prev
        for r in range(0, size, 8):
            c, i = (offset + r) // chunk, (offset + r) % chunk
            ss_x[c, i : i + 8] = grams[r : r + 8, :]
    reduce_ss.start()

    @pl.loop(1, tx + 1)
    def _(a):
        @pl.loop(1, ty + 1)
        def _(b):
            make_near(a, b)

        @pl.when(a == 1)
        def _():
            reduce_ss.second()

        @pl.when(a == 2)
        def _():
            reduce_ss.third()

        @pl.when(a == 3)
        def _():
            reduce_ss.finish()

    halo_wait(ppad, pos_s, pos_r)
    halo_wait(vpad, v1_s, v1_r)

    @pl.loop(0, tx + 2)
    def _(a):
        @pl.loop(0, ty + 2)
        def _(b):
            @pl.when(jnp.logical_not(interior(a, b)))
            def _():
                make_near(a, b)

    def products(base, x, extra):
        grams[0:width, :] = jnp.zeros((width, full), F32)
        if extra:
            grams[width : 2 * width, :] = jnp.zeros((width, full), F32)

        @pl.loop(0, tiles)
        def _(t):
            image = span[t, pl.ds(base, width)]
            grams[0:width, :] = grams[0:width, :] + dot_nt(image, span[t, 0:full])
            if extra:
                grams[width : 2 * width, 0:width] = (
                    grams[width : 2 * width, 0:width] + dot_nt(image, image))
        chunk = x.shape[1]
        for c in range(nq):
            x[c, :, 0:full] = grams[c * chunk : (c + 1) * chunk, :]
            if extra:
                x[c, :, full : full + 128] = grams[
                    width + c * chunk : width + (c + 1) * chunk, 0:128]

    products(prev, r1_x, False)
    reduce_1.start()
    reduce_1.second()
    reduce_1.third()
    reduce_1.finish()

    chunk = ss_x.shape[1]
    grams[prev : prev + width, :] = jnp.zeros((width, full), F32)
    for r in range(0, prev + width, 8):
        c, i = r // chunk, r % chunk
        row = r if r < prev else r + width
        grams[row : row + 8, :] = ss_y[c, i : i + 8]
    lane = lax.broadcasted_iota(jnp.int32, (width, full), 1)
    inside = (lane >= prev) & (lane < prev + width)
    tlane = lax.broadcasted_iota(jnp.int32, (full, full), 1)
    grams[...] = jnp.where((tlane >= prev) & (tlane < prev + width), 0.0, grams[...])

    red = jnp.concatenate([r1_y[c] for c in range(nq)], axis=0)
    coef = jnp.where(inside, 0.0, red)
    over = dot_nn(coef, grams[...])
    gram = red[:, prev : prev + width] + dot_nt(over - 2.0 * coef, coef)
    lower = inverse_factor(gram)
    mix[:, 0:full] = -dot_nn(lower, coef)
    mix[:, prev : prev + width] = lower
    cross = dot_nn(lower, coef - over)

    @pl.loop(0, tiles)
    def _(t):
        fresh = dot_nn(mix[:, 0:full], span[t, 0:full])
        first_out[t] = fresh
        span[t, pl.ds(prev, width)] = fresh
        vpad[t // ty + 1, lax.rem(t, ty) + 1] = fresh

    halo_start(vpad, v2_s, v2_r)
    rowi = lax.broadcasted_iota(jnp.int32, (width, full), 0)
    cross = jnp.where(lane == rowi + prev, 1.0, cross)
    cross_t = jnp.transpose(cross)
    grams[prev : prev + width, :] = cross
    grams[:, prev : prev + width] = cross_t
    tmat = grams[...]

    def second_apply(inner):
        @pl.loop(0, tiles)
        def _(t):
            oa, ob = t // ty + 1, lax.rem(t, ty) + 1
            for code in range(9):
                na, nb = oa + code // 3 - 1, ob + code % 3 - 1
                use = interior(na, nb) if inner else jnp.logical_not(interior(na, nb))

                @pl.when(use)
                def _(na=na, nb=nb, code=code):
                    apply_block(na, nb, t * 9 + code, t, prev + 2 * width)

    def split_all(inner):
        @pl.loop(0, tx + 2)
        def _(a):
            @pl.loop(0, ty + 2)
            def _(b):
                use = interior(a, b) if inner else jnp.logical_not(interior(a, b))

                @pl.when(use)
                def _():
                    split(a, b)

    mix[:, full : full + 128] = jnp.zeros((width, 128), F32)
    ss_keep = tmat
    split_all(True)
    second_apply(True)
    halo_wait(vpad, v2_s, v2_r)
    split_all(False)
    second_apply(False)

    products(prev + 2 * width, r2_x, True)
    grams[...] = ss_keep
    reduce_2.start()
    reduce_2.second()
    reduce_2.third()
    reduce_2.finish()
    red = jnp.concatenate([r2_y[c] for c in range(nq)], axis=0)
    coef = red[:, 0:full]
    over = dot_nn(coef, grams[...])
    gram = red[:, full : full + width] + dot_nt(over - 2.0 * coef, coef)
    lower = inverse_factor(gram)
    mix[:, 0:full] = -dot_nn(lower, coef)
    mix[:, full : full + width] = lower

    @pl.loop(0, tiles)
    def _(t):
        second_out[t] = dot_nn(mix[:, 0:full], span[t, 0:full]) + dot_nn(
            mix[:, full : full + width], span[t, full : full + width])


def on_device(nsx, nsy, nsz, prior, current, site_xy, links):
    prev, tx, ty, ts = prior.shape
    width = current.shape[0]
    tiles = tx * ty
    nq = nsy * nsz
    full = prev + 2 * width

    def tiled(x):
        return jnp.transpose(x.reshape(x.shape[0], tiles, ts), (1, 0, 2))

    def reduce_bufs(rows, cols):
        chunk = rows // nq
        return [
            pltpu.VMEM((nq, chunk, cols), F32),
            pltpu.VMEM((nq - 1, chunk, cols), F32),
            pltpu.VMEM((nsx, chunk, cols), F32),
            pltpu.VMEM((chunk, cols), F32),
            pltpu.VMEM((nq, chunk, cols), F32),
        ]

    dma = pltpu.SemaphoreType.DMA
    first, second = pl.pallas_call(
        functools.partial(body, nsx, nsy, nsz, tx, ty),
        out_shape=[jax.ShapeDtypeStruct((tiles, width, ts), F32)] * 2,
        in_specs=[
            pl.BlockSpec(memory_space=pltpu.SMEM),
            pl.BlockSpec(memory_space=pl.ANY),
            pl.BlockSpec(memory_space=pl.ANY),
            pl.BlockSpec(memory_space=pl.ANY),
        ],
        out_specs=[pl.BlockSpec(memory_space=pltpu.VMEM)] * 2,
        scratch_shapes=[
            pltpu.VMEM((tiles * 9, ts, ts), BF16),
            pltpu.VMEM((tiles * 9, ts, ts), BF16),
            pltpu.VMEM((tiles, full + width, ts), F32),
            pltpu.VMEM((tx + 2, ty + 2, width, ts), F32),
            pltpu.VMEM((tx + 2, ty + 2, 2 * width, ts), BF16),
            pltpu.VMEM((tx + 2, ty + 2, 2, ts), F32),
            pltpu.VMEM((2, ts, 128), F32),
            pltpu.VMEM((full, full), F32),
            pltpu.VMEM((width, full + 128), F32),
        ]
        + reduce_bufs(prev + width, full)
        + reduce_bufs(width, full)
        + reduce_bufs(width, full + 128)
        + [dma((2 * tx + 2,))]
        + [dma((8,))] * 6
        + [dma((3, nq - 1))] * 2
        + [dma((3, nsx - 1))] * 2
        + [dma((3, nq - 1))] * 2,
        compiler_params=pltpu.CompilerParams(
            collective_id=0, has_side_effects=True, vmem_limit_bytes=62 * 1024 * 1024),
    )(links.reshape(-1), tiled(prior), tiled(current), tiled(site_xy))

    def untiled(x):
        return jnp.transpose(x, (1, 0, 2)).reshape(width, tx, ty, ts)

    return untiled(first), untiled(second)


def solution(mesh):
    sizes = mesh.shape
    whole = P(None, ("groups", "sx"), ("sy", "sz"), None)
    return jax.shard_map(
        functools.partial(on_device, sizes["sx"], sizes["sy"], sizes["sz"]),
        mesh=mesh,
        in_specs=(whole, whole, whole, P(None, ("groups", "sx"), ("sy", "sz"))),
        out_specs=(whole, whole),
        check_vma=False,
    )
```

time: 540 us -> 169 us (0.31); the launches traced: 532 us -> 169 us
  blocking collectives: 183 us -> 0 us
  matrix products: 155 us -> 0 us
  Pallas kernels: 0 us -> 155 us
  waiting for transfers between devices: 87.3 us -> 0 us
  starting transfers between devices: 28.6 us -> 0 us
  other arithmetic: 27.3 us -> 0 us
  local copies, waits for them, and re-layouts: 35.5 us -> 13 us
  between operations: 15.3 us -> 0.66 us
    psum x3 -> x0, blocking collectives: 183 us -> none  [the longest x2 118 us: lanczos_step(): lax.psum(inner(flat_image, flat_image), ('sx', 'sy', 'sz')) / sites_total]
    pallas_call x0 -> x1, Pallas kernels: none -> 155 us  [on_device(): pl.pallas_call(functools.partial(body, nsx, nsy, nsz, tx, ty), out_shape=...]
    dot_general x24 -> x0, matrix products: 150 us -> none  [the longest x18 128 us: coupling(): jnp.einsum('xyij,mxyj->mxyi', weights[code], near, precision=lax.Precisio...]
    psum x1 -> x0, waiting for transfers between devices: 86.5 us -> none  [lanczos_step(): lax.psum(inner(flat_span, flat_image), ('sx', 'sy', 'sz')) / sites_total]
    ppermute x12 -> x0, starting transfers between devices: 28.5 us -> none  [the longest x6 20.6 us: extended(): lax.ppermute(lax.slice_in_dim(block, block.shape[dim] - width, None, axis...]
    another operation x10 -> x0, other arithmetic: 24.1 us -> none  [the longest x6 13.1 us: lanczos_step(): lower = jnp.linalg.cholesky(gram)]
    reshape x6 -> x1, local copies, waits for them, and re-layouts: 15.5 us -> 0.7 us  [on_device(): links.reshape(-1)]
    another operation x2 -> x0, matrix products: 5.52 us -> none  [lower_solve(): return lax.linalg.triangular_solve(lower, rhs, left_side=True, lower=True)]
  transfers between devices with their start and end apart: 13 -> 0, of which waited for: 2 -> 0; matrix products, arithmetic and copies ran while one was open for 14% -> 0% of each run, Pallas kernels for 0% -> 0%
where the time goes in v1:
time: 169 us
  Pallas kernels  155 us (92%)
  local copies, waits for them, and re-layouts  13 us (8%)
    pallas_call x1, Pallas kernels, on_device(): pl.pallas_call(functools.partial(body, nsx, nsy, nsz, tx, ty), out_shape=...  155 us
    unnamed x10, local copies, waits for them, and re-layouts  12.3 us

profile of v1, /device:TPU:0, one launch (start us, length us, event | category | flops | bytes accessed | tf_op | source)
XLA Modules:
  0.0 168.7 jit_solution(3953878344307939968)
XLA Ops:
  0.6 0.0 copy-start
  0.6 1.0 copy.11
  1.6 0.7 reshape.22.links
  2.3 1.4 copy.14
  3.7 2.8 %copy.13 = f32[64,4,4,256]{3,0,2,1:T(8,128)} copy(f32[64,4,4,256]{3,2,1,0:T(4,128)} %param.5) | data formatting | bytes 2097152 | tf_op args[1]
  6.5 0.0 copy-done
  6.5 2.6 %copy.12 = f32[128,4,4,256]{3,0,2,1:T(8,128)} copy(f32[128,4,4,256]{3,2,1,0:T(4,128)S(1)} %copy-done) | data formatting | bytes 4194304 | tf_op args[0]
  9.1 155.0 %shard_map.59 = (f32[16,64,256]{2,1,0:T(8,128)}, f32[16,64,256]{2,1,0:T(8,128)}) custom-call(s32[144]{0:T(256)} %reshape.22.links, f32[16,128,256]{2,1,0:T(8,128)} %bitcast.15, f32[16,64,256]{2,1,0:T(8,128)} %bitcast.16, f32[16,2,256]{2,1,0:T(2,128)} %bitcast.19), custom_call_target="tpu_custom_call" | custom-call | tf_op jit(solution)/shard_map/pallas_call | solution.py:459
  164.1 0.0 copy-start.1
  164.1 3.0 %copy.15 = f32[64,4,4,256]{3,2,1,0:T(4,128)} copy(f32[64,4,4,256]{3,0,2,1:T(8,128)} %bitcast.18) | data formatting | bytes 2097152
  167.1 0.0 copy-done.1
  167.1 1.6 copy.16
Async XLA Ops:
  0.6 5.9 %copy-start = (f32[128,4,4,256]{3,2,1,0:T(4,128)S(1)}, f32[128,4,4,256]{3,2,1,0:T(4,128)}, u32[]{:S(2)}) copy-start(f32[128,4,4,256]{3,2,1,0:T(4,128)} %param.4) | copy-start | bytes 6291460
  164.1 3.0 %copy-start.1 = (f32[16,64,256]{2,1,0:T(8,128)S(1)}, f32[16,64,256]{2,1,0:T(8,128)}, u32[]{:S(2)}) copy-start(f32[16,64,256]{2,1,0:T(8,128)} %get-tuple-element.5) | copy-start | bytes 3145732

commit v2 on v1

v2 whole, which is shorter than its diff:
```python
import functools

import jax
import jax.numpy as jnp
from jax import lax
from jax.experimental import pallas as pl
from jax.experimental.pallas import tpu as pltpu
from jax.sharding import PartitionSpec as P

GAIN = 0.0625
MESH = pl.DeviceIdType.MESH
F32 = jnp.float32
BF16 = jnp.bfloat16
HIGH = lax.Precision.HIGHEST
DIRS = [(da, db) for da in (-1, 0, 1) for db in (-1, 0, 1) if (da, db) != (0, 0)]


def dot_nn(left, right):
    return lax.dot_general(
        left, right, (((1,), (0,)), ((), ())), precision=HIGH, preferred_element_type=F32
    )


def dot_nt(left, right):
    return lax.dot_general(
        left, right, (((1,), (1,)), ((), ())), precision=HIGH, preferred_element_type=F32
    )


def dot_fast(left, right):
    return lax.dot_general(
        left, right, (((1,), (0,)), ((), ())), preferred_element_type=F32
    )


def dot_fast_nt(left, right):
    return lax.dot_general(
        left, right, (((1,), (1,)), ((), ())), preferred_element_type=F32
    )


def halves(value):
    high = value.astype(BF16)
    return high, (value - high.astype(F32)).astype(BF16)


def thirds(value):
    one = value.astype(BF16).astype(F32)
    rest = value - one
    two = rest.astype(BF16).astype(F32)
    return one, two, rest - two


def inverse_factor(gram):
    size = gram.shape[0]
    rows = lax.broadcasted_iota(jnp.int32, (size, size), 0)
    cols = lax.broadcasted_iota(jnp.int32, (size, size), 1)
    eye = jnp.where(rows == cols, 1.0, 0.0).astype(F32)
    work = jnp.concatenate([eye, gram], axis=1)
    wide = 2 * size
    rowid = lax.broadcasted_iota(jnp.int32, (size, wide), 0)
    pivots = jnp.ones((size, wide), F32)
    panel = 8
    for base in range(0, size, panel):
        cast = [
            jnp.broadcast_to(work[:, size + base + c : size + base + c + 1], (size, wide))
            for c in range(panel)
        ]
        for c in range(panel):
            k = base + c
            pivot = cast[c][k : k + 1, :]
            pivots = jnp.where(rowid == k, pivot, pivots)
            factor = jnp.where(rowid > k, cast[c] * (1.0 / pivot), 0.0)
            work = work - factor * work[k : k + 1, :]
            for d in range(c + 1, panel):
                cast[d] = cast[d] - factor * cast[d][k : k + 1, :]
    scaled = work * lax.rsqrt(pivots)
    return scaled[:, :size]


def body(
    nsx, nsy, nsz, tx, ty,
    links, prior_in, cur_in, pos_in,
    first_out, second_out,
    khi, klo, shi, slo, vpad, vbf, ppad, rowbuf, near_m, own_m, stage, image, grams, skew,
    ss_x, ss_a, ss_b, ss_z, ss_y,
    r1_x, r1_a, r1_b, r1_z, r1_y,
    r2_x, r2_a, r2_b, r2_z, r2_y,
    cur_sem, pos_sem, prior_sem, out_sem, pos_s, pos_r, v1_s, v1_r, v2_s, v2_r, pl_s, pl_r, z_s, z_r, g_s, g_r,
):
    nq = nsy * nsz
    group = lax.axis_index("groups")
    sx = lax.axis_index("sx")
    q = lax.axis_index("sy") * nsz + lax.axis_index("sz")
    prev = prior_in.shape[0]
    width = cur_in.shape[0]
    full = prev + 2 * width
    total_sites = float(tx * ty * 256 * nsx * nq)
    tiles = tx * ty

    def device(s, p):
        return (group, s, p // nsz, lax.rem(p, nsz))

    def exists(d):
        s, p = sx + d[0], q + d[1]
        return (s >= 0) & (s < nsx) & (p >= 0) & (p < nq)

    loads, prior_loads = [], []
    for t in range(tiles):
        a, b = t // ty, t % ty
        loads.append(pltpu.make_async_copy(
            pos_in.at[:, a, b], ppad.at[a + 1, b + 1], pos_sem.at[t]))
        loads.append(pltpu.make_async_copy(
            cur_in.at[:, a, b], vpad.at[a + 1, b + 1], cur_sem.at[t]))
        for h in range(prev // width):
            prior_loads.append(pltpu.make_async_copy(
                prior_in.at[pl.ds(h * width, width), a, b], stage.at[h, t],
                prior_sem.at[h, t]))
    for a in range(tx + 2):
        for b in range(ty + 2):
            if a in (0, tx + 1) or b in (0, ty + 1):
                vpad[a, b] = jnp.zeros((width, 256), F32)
                ppad[a, b] = jnp.zeros((2, 256), F32)
    for load in loads:
        load.start()
    for load in prior_loads:
        load.start()

    barrier = pltpu.get_barrier_semaphore()
    expected = jnp.int32(nq - 1 + nsx - 1)
    for d in DIRS:
        ok = exists(d)
        expected = expected + jnp.where(ok, 1, 0)

        @pl.when(ok)
        def _(d=d):
            pl.semaphore_signal(
                barrier, inc=1, device_id=device(sx + d[0], q + d[1]), device_id_type=MESH)
    for k in range(1, nq):
        pl.semaphore_signal(
            barrier, inc=1, device_id=device(sx, lax.rem(q + k, nq)), device_id_type=MESH)
    for k in range(1, nsx):
        pl.semaphore_signal(
            barrier, inc=1, device_id=device(lax.rem(sx + k, nsx), q), device_id_type=MESH)
    pl.semaphore_wait(barrier, expected)
    for load in loads:
        load.wait()

    def pick(shift, count):
        src = {-1: pl.ds(1, 1), 0: pl.ds(1, count), 1: pl.ds(count, 1)}[shift]
        dst = {-1: pl.ds(count + 1, 1), 0: pl.ds(1, count), 1: pl.ds(0, 1)}[shift]
        return src, dst

    def halo_copy(ref, i, send, recv):
        d = DIRS[i]
        (sa, da), (sb, db) = pick(d[0], tx), pick(d[1], ty)
        return pltpu.make_async_remote_copy(
            src_ref=ref.at[sa, sb], dst_ref=ref.at[da, db],
            send_sem=send.at[i], recv_sem=recv.at[i],
            device_id=device(sx + d[0], q + d[1]), device_id_type=MESH)

    def halo_start(ref, send, recv):
        for i, d in enumerate(DIRS):
            @pl.when(exists(d))
            def _(i=i):
                halo_copy(ref, i, send, recv).start()

    def halo_wait(ref, send, recv):
        for i, d in enumerate(DIRS):
            @pl.when(exists(d))
            def _(i=i):
                halo_copy(ref, i, send, recv).wait_send()

            @pl.when(exists((-d[0], -d[1])))
            def _(i=i):
                halo_copy(ref, i, send, recv).wait_recv()

    class Reduce:
        def __init__(self, which, x, a, b, z, y):
            self.w, self.x, self.a, self.b, self.z, self.y = which, x, a, b, z, y

        def plane(self, k):
            to = lax.rem(q + k, nq)
            return pltpu.make_async_remote_copy(
                src_ref=self.x.at[to], dst_ref=self.a.at[k - 1],
                send_sem=pl_s.at[self.w, k - 1], recv_sem=pl_r.at[self.w, k - 1],
                device_id=device(sx, to), device_id_type=MESH)

        def line(self, k):
            to = lax.rem(sx + k, nsx)
            return pltpu.make_async_remote_copy(
                src_ref=self.z, dst_ref=self.b.at[sx],
                send_sem=z_s.at[self.w, k - 1], recv_sem=z_r.at[self.w, k - 1],
                device_id=device(to, q), device_id_type=MESH)

        def back(self, k):
            to = lax.rem(q + k, nq)
            return pltpu.make_async_remote_copy(
                src_ref=self.y.at[q], dst_ref=self.y.at[q],
                send_sem=g_s.at[self.w, k - 1], recv_sem=g_r.at[self.w, k - 1],
                device_id=device(sx, to), device_id_type=MESH)

        def start(self):
            for k in range(1, nq):
                self.plane(k).start()

        def second(self):
            for k in range(1, nq):
                self.plane(k).wait()
            part = self.x[q]
            for k in range(1, nq):
                part = part + self.a[k - 1]
            self.z[...] = part
            for k in range(1, nsx):
                self.line(k).start()
            self.b[sx] = part

        def third(self):
            for k in range(1, nsx):
                self.line(k).wait()
            part = self.b[0]
            for k in range(1, nsx):
                part = part + self.b[k]
            self.y[q] = part * (1.0 / total_sites)
            for k in range(1, nq):
                self.back(k).start()

        def finish(self):
            for k in range(1, nq):
                self.back(k).wait()

    reduce_ss = Reduce(0, ss_x, ss_a, ss_b, ss_z, ss_y)
    reduce_1 = Reduce(1, r1_x, r1_a, r1_b, r1_z, r1_y)
    reduce_2 = Reduce(2, r2_x, r2_a, r2_b, r2_z, r2_y)

    halo_start(ppad, pos_s, pos_r)
    halo_start(vpad, v1_s, v1_r)

    def split(a, b):
        high, low = halves(vpad[a, b])
        vbf[a, b, 0:width] = high
        vbf[a, b, width : 2 * width] = low
        return high, low

    def interior(a, b):
        return (a >= 1) & (a <= tx) & (b >= 1) & (b <= ty)

    def outer(fn):
        @pl.loop(0, tx + 2)
        def _(a):
            @pl.loop(0, ty + 2)
            def _(b):
                @pl.when(jnp.logical_not(interior(a, b)))
                def _():
                    fn(a, b)

    first_rows = pl.ds(prev, width)
    cur_rows = pl.ds(prev + width, width)
    second_rows = pl.ds(prev + 2 * width, width)

    for load in prior_loads:
        load.wait()
    grams[...] = jnp.zeros_like(grams)
    skew[...] = jnp.zeros_like(skew)

    @pl.loop(0, tiles)
    def _(t):
        for h in range(prev // width):
            high, low = halves(stage[h, t])
            shi[t, h * width : (h + 1) * width] = high
            slo[t, h * width : (h + 1) * width] = low
        high, low = split(t // ty + 1, lax.rem(t, ty) + 1)
        shi[t, cur_rows] = high
        slo[t, cur_rows] = low
        shi[t, first_rows] = jnp.zeros((width, 256), BF16)
        slo[t, first_rows] = jnp.zeros((width, 256), BF16)

    group_size = 4

    @pl.loop(0, tiles // group_size)
    def _(i):
        high = [shi[i * group_size + n, 0:full] for n in range(group_size)]
        low = [slo[i * group_size + n, 0:full] for n in range(group_size)]
        grams[...] = grams[...] + sum(dot_fast_nt(h, h) for h in high)
        skew[...] = skew[...] + sum(dot_fast_nt(h, l) for h, l in zip(high, low))
    grams[...] = grams[...] + skew[...] + jnp.transpose(skew[...])
    chunk = ss_x.shape[1]
    for r in range(0, prev + width, 8):
        c, i = r // chunk, r % chunk
        row = r if r < prev else r + width
        ss_x[c, i : i + 8] = grams[row : row + 8, :]
    reduce_ss.start()

    rowbuf[...] = jnp.zeros_like(rowbuf)

    def place_terms(slot, terms):
        for k, term in enumerate(terms):
            if term is not None:
                rowbuf[slot, k : k + 1, :] = term

    def near_factors(a, b):
        x, y = ppad[a, b, 0:1, :], ppad[a, b, 1:2, :]
        xs, ys, norm = thirds(x), thirds(y), thirds(x * x + y * y)
        one = jnp.ones((1, 256), F32)
        terms = [*norm, one, one, one]
        for p in (xs, ys):
            terms += [p[0], p[0], p[1], p[1], p[0], p[2]]
        place_terms(0, terms)
        near_m[a, b] = jnp.transpose(rowbuf[0]).astype(BF16)

    def own_factors(oa, ob):
        for code in range(9):
            da, db = code // 3 - 1, code % 3 - 1
            x = ppad[oa, ob, 0:1, :] - float(da)
            y = ppad[oa, ob, 1:2, :] - float(db)
            xs, ys, norm = thirds(x), thirds(y), thirds(x * x + y * y)
            one = jnp.ones((1, 256), F32)
            terms = [one, one, one, *norm]
            for p in (xs, ys):
                terms += [-2.0 * p[n] for n in (0, 1, 0, 1, 2, 0)]
            place_terms(code, terms)
            own_m[code] = rowbuf[code].astype(BF16)

    @pl.loop(0, tiles)
    def _(t):
        near_factors(t // ty + 1, lax.rem(t, ty) + 1)

    halo_wait(ppad, pos_s, pos_r)
    outer(near_factors)
    halo_wait(vpad, v1_s, v1_r)
    outer(split)

    def make_weights(t, code):
        oa, ob = t // ty + 1, lax.rem(t, ty) + 1
        na, nb = oa + code // 3 - 1, ob + code % 3 - 1
        link = links[code, t // ty, lax.rem(t, ty)].astype(F32) * GAIN
        c4 = link * 4.0
        place = t * 9 + code
        step = 64
        for j in range(0, 256, step):
            sq = dot_fast(near_m[na, nb, j : j + step, :], own_m[code])
            sq = jnp.maximum(sq, 1e-12)
            dist = sq * lax.rsqrt(sq)
            fall = jnp.maximum(1.0 - dist, 0.0)
            two = fall * fall
            high, low = halves((two * two) * (dist * c4 + link))
            khi[place, j : j + step, :] = high
            klo[place, j : j + step, :] = low

    def apply_tile(t, rows):
        oa, ob = t // ty + 1, lax.rem(t, ty) + 1
        both, part = None, None
        for code in range(9):
            na, nb = oa + code // 3 - 1, ob + code % 3 - 1
            one = dot_fast(vbf[na, nb], khi[t * 9 + code])
            two = dot_fast(vbf[na, nb, 0:width], klo[t * 9 + code])
            both = one if both is None else both + one
            part = two if part is None else part + two
        high, low = halves(both[0:width] + both[width : 2 * width] + part)
        shi[t, rows] = high
        slo[t, rows] = low

    @pl.loop(0, tiles)
    def _(t):
        own_factors(t // ty + 1, lax.rem(t, ty) + 1)
        for code in range(9):
            make_weights(t, code)
        apply_tile(t, first_rows)

        @pl.when(t == 3)
        def _():
            reduce_ss.second()

        @pl.when(t == 7)
        def _():
            reduce_ss.third()

        @pl.when(t == 11)
        def _():
            reduce_ss.finish()

    def products(rows, extra):
        image[...] = jnp.zeros_like(image)

        @pl.loop(0, tiles // group_size)
        def _(i):
            total, mine = None, None
            for n in range(group_size):
                t = i * group_size + n
                high, low = shi[t, rows], slo[t, rows]
                both = jnp.concatenate([high, low], axis=0)
                one = dot_fast_nt(both, shi[t, 0:full])
                one = one[0:width] + one[width : 2 * width] + dot_fast_nt(high, slo[t, 0:full])
                total = one if total is None else total + one
                if extra:
                    one = dot_fast_nt(both, high)
                    one = one[0:width] + one[width : 2 * width] + dot_fast_nt(high, low)
                    mine = one if mine is None else mine + one
            image[:, 0:full] = image[:, 0:full] + total
            if extra:
                image[:, full : full + width] = image[:, full : full + width] + mine

    def reduce_now(reduce, columns):
        chunk = reduce.x.shape[1]
        for c in range(nq):
            reduce.x[c] = image[c * chunk : (c + 1) * chunk, 0:columns]
        reduce.start()
        reduce.second()
        reduce.third()
        reduce.finish()
        return jnp.concatenate([reduce.y[c] for c in range(nq)], axis=0)

    products(first_rows, False)
    chunk = ss_x.shape[1]
    grams[prev : prev + width, :] = jnp.zeros((width, full), F32)
    for r in range(0, prev + width, 8):
        c, i = r // chunk, r % chunk
        row = r if r < prev else r + width
        grams[row : row + 8, :] = ss_y[c, i : i + 8]
    lane = lax.broadcasted_iota(jnp.int32, (width, full), 1)
    inside = (lane >= prev) & (lane < prev + width)
    tlane = lax.broadcasted_iota(jnp.int32, (full, full), 1)
    grams[...] = jnp.where((tlane >= prev) & (tlane < prev + width), 0.0, grams[...])

    red = reduce_now(reduce_1, full)
    coef = jnp.where(inside, 0.0, red)
    over = dot_nn(coef, grams[...])
    gram = red[:, prev : prev + width] + dot_nt(over - 2.0 * coef, coef)
    lower = inverse_factor(gram)
    image[:, 0:full] = -dot_nn(lower, coef)
    image[:, prev : prev + width] = lower
    cross = dot_nn(lower, coef - over)
    mix_high, mix_low = halves(image[:, 0:full])
    mix = jnp.concatenate([mix_high, mix_low], axis=0)

    def mixed(mix, mix_high, high, low):
        both = dot_fast(mix, high)
        return both[0:width] + both[width : 2 * width] + dot_fast(mix_high, low)

    def first_copy(t):
        a, b = t // ty, lax.rem(t, ty)
        return pltpu.make_async_copy(
            vpad.at[a + 1, b + 1], first_out.at[:, a, b], out_sem.at[0, t])

    def second_copy(t):
        a, b = t // ty, lax.rem(t, ty)
        return pltpu.make_async_copy(
            stage.at[0, t], second_out.at[:, a, b], out_sem.at[1, t])

    @pl.loop(0, tiles // group_size)
    def _(i):
        for n in range(group_size):
            t = i * group_size + n
            a, b = t // ty + 1, lax.rem(t, ty) + 1
            fresh = mixed(mix, mix_high, shi[t, 0:full], slo[t, 0:full])
            vpad[a, b] = fresh
            high, low = halves(fresh)
            shi[t, first_rows] = high
            slo[t, first_rows] = low
            vbf[a, b, 0:width] = high
            vbf[a, b, width : 2 * width] = low

    halo_start(vpad, v2_s, v2_r)

    @pl.loop(0, tiles)
    def _(t):
        first_copy(t).start()
    rowi = lax.broadcasted_iota(jnp.int32, (width, full), 0)
    cross = jnp.where(lane == rowi + prev, 1.0, cross)
    grams[prev : prev + width, :] = cross
    grams[:, prev : prev + width] = jnp.transpose(cross)

    def inner(t):
        a, b = t // ty, lax.rem(t, ty)
        return (a >= 1) & (a < tx - 1) & (b >= 1) & (b < ty - 1)

    @pl.loop(0, tiles)
    def _(t):
        @pl.when(inner(t))
        def _():
            apply_tile(t, second_rows)
    halo_wait(vpad, v2_s, v2_r)
    outer(split)

    @pl.loop(0, tiles)
    def _(t):
        @pl.when(jnp.logical_not(inner(t)))
        def _():
            apply_tile(t, second_rows)

    products(second_rows, True)
    red = reduce_now(reduce_2, full + 128)
    coef = red[:, 0:full]
    over = dot_nn(coef, grams[...])
    gram = red[:, full : full + width] + dot_nt(over - 2.0 * coef, coef)
    lower = inverse_factor(gram)
    main_high, main_low = halves(-dot_nn(lower, coef))
    tail_high, tail_low = halves(lower)
    main = jnp.concatenate([main_high, main_low], axis=0)
    tail = jnp.concatenate([tail_high, tail_low], axis=0)

    @pl.loop(0, tiles // group_size)
    def _(i):
        for n in range(group_size):
            t = i * group_size + n
            stage[0, t] = mixed(main, main_high, shi[t, 0:full], slo[t, 0:full]) + mixed(
                tail, tail_high, shi[t, second_rows], slo[t, second_rows])
            second_copy(t).start()

    @pl.loop(0, tiles)
    def _(t):
        first_copy(t).wait()
        second_copy(t).wait()


def on_device(nsx, nsy, nsz, prior, current, site_xy, links):
    prev, tx, ty, ts = prior.shape
    width = current.shape[0]
    tiles = tx * ty
    nq = nsy * nsz
    full = prev + 2 * width

    def reduce_bufs(rows, cols):
        chunk = rows // nq
        return [
            pltpu.VMEM((nq, chunk, cols), F32),
            pltpu.VMEM((nq - 1, chunk, cols), F32),
            pltpu.VMEM((nsx, chunk, cols), F32),
            pltpu.VMEM((chunk, cols), F32),
            pltpu.VMEM((nq, chunk, cols), F32),
        ]

    dma = pltpu.SemaphoreType.DMA
    first, second = pl.pallas_call(
        functools.partial(body, nsx, nsy, nsz, tx, ty),
        out_shape=[jax.ShapeDtypeStruct(current.shape, F32)] * 2,
        in_specs=[
            pl.BlockSpec(memory_space=pltpu.SMEM),
            pl.BlockSpec(memory_space=pl.ANY),
            pl.BlockSpec(memory_space=pl.ANY),
            pl.BlockSpec(memory_space=pl.ANY),
        ],
        out_specs=[pl.BlockSpec(memory_space=pl.ANY)] * 2,
        scratch_shapes=[
            pltpu.VMEM((tiles * 9, ts, ts), BF16),
            pltpu.VMEM((tiles * 9, ts, ts), BF16),
            pltpu.VMEM((tiles, full + width, ts), BF16),
            pltpu.VMEM((tiles, full + width, ts), BF16),
            pltpu.VMEM((tx + 2, ty + 2, width, ts), F32),
            pltpu.VMEM((tx + 2, ty + 2, 2 * width, ts), BF16),
            pltpu.VMEM((tx + 2, ty + 2, 2, ts), F32),
            pltpu.VMEM((9, 32, ts), F32),
            pltpu.VMEM((tx + 2, ty + 2, ts, 32), BF16),
            pltpu.VMEM((9, 32, ts), BF16),
            pltpu.VMEM((prev // width, tiles, width, ts), F32),
            pltpu.VMEM((width, full + 128), F32),
            pltpu.VMEM((full, full), F32),
            pltpu.VMEM((full, full), F32),
        ]
        + reduce_bufs(prev + width, full)
        + reduce_bufs(width, full)
        + reduce_bufs(width, full + 128)
        + [dma((tiles,))] * 2
        + [dma((prev // width, tiles)), dma((2, tiles))]
        + [dma((8,))] * 6
        + [dma((3, nq - 1))] * 2
        + [dma((3, nsx - 1))] * 2
        + [dma((3, nq - 1))] * 2,
        compiler_params=pltpu.CompilerParams(
            collective_id=0, has_side_effects=True, vmem_limit_bytes=62 * 1024 * 1024),
    )(links, prior, current, site_xy)
    return first, second


def solution(mesh):
    sizes = mesh.shape
    whole = P(None, ("groups", "sx"), ("sy", "sz"), None)
    return jax.shard_map(
        functools.partial(on_device, sizes["sx"], sizes["sy"], sizes["sz"]),
        mesh=mesh,
        in_specs=(whole, whole, whole, P(None, ("groups", "sx"), ("sy", "sz"))),
        out_specs=(whole, whole),
        check_vma=False,
    )
```

time: 169 us -> 101 us (0.60)
  Pallas kernels: 155 us -> 95.6 us
  local copies, waits for them, and re-layouts: 13 us -> 4.85 us
    pallas_call x1, Pallas kernels: 155 us -> 95.6 us  [on_device(): pl.pallas_call(functools.partial(body, nsx, nsy, nsz, tx, ty), out_shape=...]
    unnamed x10 -> x5, local copies, waits for them, and re-layouts: 12.3 us -> 4.85 us
where the time goes in v2:
time: 101 us
  Pallas kernels  95.6 us (95%)
  local copies, waits for them, and re-layouts  4.85 us (5%)
    pallas_call x1, Pallas kernels, on_device(): pl.pallas_call(functools.partial(body, nsx, nsy, nsz, tx, ty), out_shape=...  95.6 us
    unnamed x5, local copies, waits for them, and re-layouts  4.85 us

profile of v2, /device:TPU:0, one launch (start us, length us, event | category | flops | bytes accessed | tf_op | source)
XLA Modules:
  0.0 101.1 jit_solution(1485725415367297515)
XLA Ops:
  0.6 1.4 %copy.6.links = s32[9,4,4]{2,1,0:T(4,128)} copy(s32[9,4,4]{0,2,1:T(4,128)} %param.7) | data formatting | bytes 1152 | tf_op args[3]
  2.0 95.6 %shard_map.59 = (f32[64,4,4,256]{3,2,1,0:T(4,128)}, f32[64,4,4,256]{3,2,1,0:T(4,128)}) custom-call(s32[9,4,4]{2,1,0:T(4,128)} %copy.6.links, f32[128,4,4,256]{3,2,1,0:T(4,128)} %prior_in.1, f32[64,4,4,256]{3,2,1,0:T(4,128)} %cur_in.1, f32[2,4,4,256]{3,2,1,0:T(4,128)} %pos_in.1), custom_call_target="tpu_custom_call" | custom-call | tf_op jit(solution)/shard_map/pallas_call | solution.py:534
  97.7 0.0 copy-start
  97.7 2.5 %copy.9 = f32[64,4,4,256]{3,2,1,0:T(4,128)} copy(f32[64,4,4,256]{3,2,1,0:T(4,128)} %get-tuple-element.4) | data formatting | bytes 2097152
  100.2 0.0 copy-done
  100.2 1.0 copy.10
Async XLA Ops:
  97.7 2.5 %copy-start = (f32[64,4,4,256]{3,2,1,0:T(4,128)S(1)}, f32[64,4,4,256]{3,2,1,0:T(4,128)}, u32[]{:S(2)}) copy-start(f32[64,4,4,256]{3,2,1,0:T(4,128)} %get-tuple-element.5) | copy-start | bytes 3145732

commit v3 on v2

--- a/solution.py
+++ b/solution.py
@@ -78,6 +78,10 @@
     return scaled[:, :size]
 
 
+def is_flat(nsx, nq):
+    return nsx * nq <= 16
+
+
 def body(
     nsx, nsy, nsz, tx, ty,
     links, prior_in, cur_in, pos_in,
@@ -89,6 +93,8 @@
     cur_sem, pos_sem, prior_sem, out_sem, pos_s, pos_r, v1_s, v1_r, v2_s, v2_r, pl_s, pl_r, z_s, z_r, g_s, g_r,
 ):
     nq = nsy * nsz
+    count = nsx * nq
+    flat = is_flat(nsx, nq)
     group = lax.axis_index("groups")
     sx = lax.axis_index("sx")
     q = lax.axis_index("sy") * nsz + lax.axis_index("sz")
@@ -127,7 +133,7 @@
         load.start()
 
     barrier = pltpu.get_barrier_semaphore()
-    expected = jnp.int32(nq - 1 + nsx - 1)
+    expected = jnp.int32(count - 1 if flat else nq - 1 + nsx - 1)
     for d in DIRS:
         ok = exists(d)
         expected = expected + jnp.where(ok, 1, 0)
@@ -136,14 +142,20 @@
         def _(d=d):
             pl.semaphore_signal(
                 barrier, inc=1, device_id=device(sx + d[0], q + d[1]), device_id_type=MESH)
-    for k in range(1, nq):
-        pl.semaphore_signal(
-            barrier, inc=1, device_id=device(sx, lax.rem(q + k, nq)), device_id_type=MESH)
-    for k in range(1, nsx):
-        pl.semaphore_signal(
-            barrier, inc=1, device_id=device(lax.rem(sx + k, nsx), q), device_id_type=MESH)
+    if flat:
+        for k in range(1, count):
+            to = lax.rem(sx * nq + q + k, count)
+            pl.semaphore_signal(
+                barrier, inc=1, device_id=device(to // nq, lax.rem(to, nq)), device_id_type=MESH)
+    else:
+        for k in range(1, nq):
+            pl.semaphore_signal(
+                barrier, inc=1, device_id=device(sx, lax.rem(q + k, nq)), device_id_type=MESH)
+        for k in range(1, nsx):
+            pl.semaphore_signal(
+                barrier, inc=1, device_id=device(lax.rem(sx + k, nsx), q), device_id_type=MESH)
     pl.semaphore_wait(barrier, expected)
-    for load in loads:
+    for load in loads[0::2]:
         load.wait()
 
     def pick(shift, count):
@@ -174,6 +186,51 @@
             @pl.when(exists((-d[0], -d[1])))
             def _(i=i):
                 halo_copy(ref, i, send, recv).wait_recv()
+
+    me = sx * nq + q
+
+    def member(p):
+        return device(p // nq, lax.rem(p, nq))
+
+    class ReduceFlat:
+        def __init__(self, which, x, a, b, z, y):
+            self.w, self.x, self.a, self.y = which, x, a, y
+
+        def scatter(self, k):
+            to = lax.rem(me + k, count)
+            return pltpu.make_async_remote_copy(
+                src_ref=self.x.at[to], dst_ref=self.a.at[k - 1],
+                send_sem=pl_s.at[self.w, k - 1], recv_sem=pl_r.at[self.w, k - 1],
+                device_id=member(to), device_id_type=MESH)
+
+        def back(self, k):
+            to = lax.rem(me + k, count)
+            return pltpu.make_async_remote_copy(
+                src_ref=self.y.at[me], dst_ref=self.y.at[me],
+                send_sem=g_s.at[self.w, k - 1], recv_sem=g_r.at[self.w, k - 1],
+                device_id=member(to), device_id_type=MESH)
+
+        def start(self):
+            for k in range(1, count):
+                self.scatter(k).start()
+
+        def second(self):
+            part = self.x[me]
+            for k in range(1, count):
+                self.scatter(k).wait_recv()
+            for k in range(1, count):
+                part = part + self.a[k - 1]
+            self.y[me] = part * (1.0 / total_sites)
+            for k in range(1, count):
+                self.back(k).start()
+
+        def third(self):
+            for k in range(1, count):
+                self.scatter(k).wait_send()
+
+        def finish(self):
+            for k in range(1, count):
+                self.back(k).wait()
 
     class Reduce:
         def __init__(self, which, x, a, b, z, y):
@@ -229,11 +286,13 @@
             for k in range(1, nq):
                 self.back(k).wait()
 
-    reduce_ss = Reduce(0, ss_x, ss_a, ss_b, ss_z, ss_y)
-    reduce_1 = Reduce(1, r1_x, r1_a, r1_b, r1_z, r1_y)
-    reduce_2 = Reduce(2, r2_x, r2_a, r2_b, r2_z, r2_y)
+    reduce_ss = (ReduceFlat if flat else Reduce)(0, ss_x, ss_a, ss_b, ss_z, ss_y)
+    reduce_1 = (ReduceFlat if flat else Reduce)(1, r1_x, r1_a, r1_b, r1_z, r1_y)
+    reduce_2 = (ReduceFlat if flat else Reduce)(2, r2_x, r2_a, r2_b, r2_z, r2_y)
 
     halo_start(ppad, pos_s, pos_r)
+    for load in loads[1::2]:
+        load.wait()
     halo_start(vpad, v1_s, v1_r)
 
     def split(a, b):
@@ -245,53 +304,28 @@
     def interior(a, b):
         return (a >= 1) & (a <= tx) & (b >= 1) & (b <= ty)
 
-    def outer(fn):
-        @pl.loop(0, tx + 2)
-        def _(a):
-            @pl.loop(0, ty + 2)
-            def _(b):
-                @pl.when(jnp.logical_not(interior(a, b)))
-                def _():
-                    fn(a, b)
+    def split_halo():
+        for b in range(ty + 2):
+            split(0, b)
+            split(tx + 1, b)
+        for a in range(1, tx + 1):
+            split(a, 0)
+            split(a, ty + 1)
 
     first_rows = pl.ds(prev, width)
     cur_rows = pl.ds(prev + width, width)
     second_rows = pl.ds(prev + 2 * width, width)
 
-    for load in prior_loads:
-        load.wait()
-    grams[...] = jnp.zeros_like(grams)
-    skew[...] = jnp.zeros_like(skew)
-
     @pl.loop(0, tiles)
     def _(t):
-        for h in range(prev // width):
-            high, low = halves(stage[h, t])
-            shi[t, h * width : (h + 1) * width] = high
-            slo[t, h * width : (h + 1) * width] = low
         high, low = split(t // ty + 1, lax.rem(t, ty) + 1)
         shi[t, cur_rows] = high
         slo[t, cur_rows] = low
         shi[t, first_rows] = jnp.zeros((width, 256), BF16)
         slo[t, first_rows] = jnp.zeros((width, 256), BF16)
 
-    group_size = 4
-
-    @pl.loop(0, tiles // group_size)
-    def _(i):
-        high = [shi[i * group_size + n, 0:full] for n in range(group_size)]
-        low = [slo[i * group_size + n, 0:full] for n in range(group_size)]
-        grams[...] = grams[...] + sum(dot_fast_nt(h, h) for h in high)
-        skew[...] = skew[...] + sum(dot_fast_nt(h, l) for h, l in zip(high, low))
-    grams[...] = grams[...] + skew[...] + jnp.transpose(skew[...])
-    chunk = ss_x.shape[1]
-    for r in range(0, prev + width, 8):
-        c, i = r // chunk, r % chunk
-        row = r if r < prev else r + width
-        ss_x[c, i : i + 8] = grams[row : row + 8, :]
-    reduce_ss.start()
-
     rowbuf[...] = jnp.zeros_like(rowbuf)
+    halo_wait(ppad, pos_s, pos_r)
 
     def place_terms(slot, terms):
         for k, term in enumerate(terms):
@@ -305,8 +339,8 @@
         terms = [*norm, one, one, one]
         for p in (xs, ys):
             terms += [p[0], p[0], p[1], p[1], p[0], p[2]]
-        place_terms(0, terms)
-        near_m[a, b] = jnp.transpose(rowbuf[0]).astype(BF16)
+        place_terms(b, terms)
+        near_m[a, b] = jnp.transpose(rowbuf[b]).astype(BF16)
 
     def own_factors(oa, ob):
         for code in range(9):
@@ -321,14 +355,41 @@
             place_terms(code, terms)
             own_m[code] = rowbuf[code].astype(BF16)
 
+    @pl.loop(0, tx + 2)
+    def _(a):
+        for b in range(ty + 2):
+            near_factors(a, b)
+
+    for load in prior_loads:
+        load.wait()
+    grams[...] = jnp.zeros_like(grams)
+    skew[...] = jnp.zeros_like(skew)
+
     @pl.loop(0, tiles)
     def _(t):
-        near_factors(t // ty + 1, lax.rem(t, ty) + 1)
-
-    halo_wait(ppad, pos_s, pos_r)
-    outer(near_factors)
+        for h in range(prev // width):
+            high, low = halves(stage[h, t])
+            shi[t, h * width : (h + 1) * width] = high
+            slo[t, h * width : (h + 1) * width] = low
+
+    group_size = 4
+
+    @pl.loop(0, tiles // group_size)
+    def _(i):
+        high = [shi[i * group_size + n, 0:full] for n in range(group_size)]
+        low = [slo[i * group_size + n, 0:full] for n in range(group_size)]
+        grams[...] = grams[...] + sum(dot_fast_nt(h, h) for h in high)
+        skew[...] = skew[...] + sum(dot_fast_nt(h, l) for h, l in zip(high, low))
+    grams[...] = grams[...] + skew[...] + jnp.transpose(skew[...])
+    chunk = ss_x.shape[1]
+    for r in range(0, prev + width, 4):
+        c, i = r // chunk, r % chunk
+        row = r if r < prev else r + width
+        ss_x[c, i : i + 4] = grams[row : row + 4, :]
+    reduce_ss.start()
+
     halo_wait(vpad, v1_s, v1_r)
-    outer(split)
+    split_halo()
 
     def make_weights(t, code):
         oa, ob = t // ty + 1, lax.rem(t, ty) + 1
@@ -402,21 +463,24 @@
 
     def reduce_now(reduce, columns):
         chunk = reduce.x.shape[1]
-        for c in range(nq):
+        chunks = reduce.x.shape[0]
+        for c in range(chunks):
             reduce.x[c] = image[c * chunk : (c + 1) * chunk, 0:columns]
         reduce.start()
         reduce.second()
         reduce.third()
         reduce.finish()
-        return jnp.concatenate([reduce.y[c] for c in range(nq)], axis=0)
+        for c in range(chunks):
+            image[c * chunk : (c + 1) * chunk, 0:columns] = reduce.y[c]
+        return image[:, 0:columns]
 
     products(first_rows, False)
     chunk = ss_x.shape[1]
     grams[prev : prev + width, :] = jnp.zeros((width, full), F32)
-    for r in range(0, prev + width, 8):
+    for r in range(0, prev + width, 4):
         c, i = r // chunk, r % chunk
         row = r if r < prev else r + width
-        grams[row : row + 8, :] = ss_y[c, i : i + 8]
+        grams[row : row + 4, :] = ss_y[c, i : i + 4]
     lane = lax.broadcasted_iota(jnp.int32, (width, full), 1)
     inside = (lane >= prev) & (lane < prev + width)
     tlane = lax.broadcasted_iota(jnp.int32, (full, full), 1)
@@ -480,7 +544,7 @@
         def _():
             apply_tile(t, second_rows)
     halo_wait(vpad, v2_s, v2_r)
-    outer(split)
+    split_halo()
 
     @pl.loop(0, tiles)
     def _(t):
@@ -521,6 +585,16 @@
     full = prev + 2 * width
 
     def reduce_bufs(rows, cols):
+        if is_flat(nsx, nq):
+            count = nsx * nq
+            chunk = rows // count
+            return [
+                pltpu.VMEM((count, chunk, cols), F32),
+                pltpu.VMEM((count - 1, chunk, cols), F32),
+                pltpu.VMEM((8, 128), F32),
+                pltpu.VMEM((8, 128), F32),
+                pltpu.VMEM((count, chunk, cols), F32),
+            ]
         chunk = rows // nq
         return [
             pltpu.VMEM((nq, chunk, cols), F32),
@@ -531,6 +605,7 @@
         ]
 
     dma = pltpu.SemaphoreType.DMA
+    peers = (nsx * nq if is_flat(nsx, nq) else nq) - 1
     first, second = pl.pallas_call(
         functools.partial(body, nsx, nsy, nsz, tx, ty),
         out_shape=[jax.ShapeDtypeStruct(current.shape, F32)] * 2,
@@ -563,9 +638,9 @@
         + [dma((tiles,))] * 2
         + [dma((prev // width, tiles)), dma((2, tiles))]
         + [dma((8,))] * 6
-        + [dma((3, nq - 1))] * 2
+        + [dma((3, peers))] * 2
         + [dma((3, nsx - 1))] * 2
-        + [dma((3, nq - 1))] * 2,
+        + [dma((3, peers))] * 2,
         compiler_params=pltpu.CompilerParams(
             collective_id=0, has_side_effects=True, vmem_limit_bytes=62 * 1024 * 1024),
     )(links, prior, current, site_xy)

time: 101 us -> 105 us (1.040)
  Pallas kernels: 95.6 us -> 99.4 us
    pallas_call x1, Pallas kernels: 95.6 us -> 99.4 us  [on_device(): pl.pallas_call(functools.partial(body, nsx, nsy, nsz, tx, ty), out_shape=...]
where the time goes in v3:
time: 105 us
  Pallas kernels  99.4 us (95%)
  local copies, waits for them, and re-layouts  4.85 us (5%)
    pallas_call x1, Pallas kernels, on_device(): pl.pallas_call(functools.partial(body, nsx, nsy, nsz, tx, ty), out_shape=...  99.4 us
    unnamed x5, local copies, waits for them, and re-layouts  4.85 us

profile of v3, /device:TPU:0, one launch (start us, length us, event | category | flops | bytes accessed | tf_op | source)
XLA Modules:
  0.0 104.9 jit_solution(10404578687741408425)
XLA Ops:
  0.6 1.4 %copy.6.links = s32[9,4,4]{2,1,0:T(4,128)} copy(s32[9,4,4]{0,2,1:T(4,128)} %param.7) | data formatting | bytes 1152 | tf_op args[3]
  2.0 99.4 %shard_map.59 = (f32[64,4,4,256]{3,2,1,0:T(4,128)}, f32[64,4,4,256]{3,2,1,0:T(4,128)}) custom-call(s32[9,4,4]{2,1,0:T(4,128)} %copy.6.links, f32[128,4,4,256]{3,2,1,0:T(4,128)} %prior_in.1, f32[64,4,4,256]{3,2,1,0:T(4,128)} %cur_in.1, f32[2,4,4,256]{3,2,1,0:T(4,128)} %pos_in.1), custom_call_target="tpu_custom_call" | custom-call | tf_op jit(solution)/shard_map/pallas_call | solution.py:609
  101.4 0.0 copy-start
  101.4 2.5 %copy.9 = f32[64,4,4,256]{3,2,1,0:T(4,128)} copy(f32[64,4,4,256]{3,2,1,0:T(4,128)} %get-tuple-element.4) | data formatting | bytes 2097152
  103.9 0.0 copy-done
  103.9 1.0 copy.10
Async XLA Ops:
  101.4 2.5 %copy-start = (f32[64,4,4,256]{3,2,1,0:T(4,128)S(1)}, f32[64,4,4,256]{3,2,1,0:T(4,128)}, u32[]{:S(2)}) copy-start(f32[64,4,4,256]{3,2,1,0:T(4,128)} %get-tuple-element.5) | copy-start | bytes 3145732

commit v4 on v3

--- a/solution.py
+++ b/solution.py
@@ -79,7 +79,7 @@
 
 
 def is_flat(nsx, nq):
-    return nsx * nq <= 16
+    return nsx * nq <= 4
 
 
 def body(
@@ -388,8 +388,9 @@
         ss_x[c, i : i + 4] = grams[row : row + 4, :]
     reduce_ss.start()
 
-    halo_wait(vpad, v1_s, v1_r)
-    split_halo()
+    def inner(t):
+        a, b = t // ty, lax.rem(t, ty)
+        return (a >= 1) & (a < tx - 1) & (b >= 1) & (b < ty - 1)
 
     def make_weights(t, code):
         oa, ob = t // ty + 1, lax.rem(t, ty) + 1
@@ -426,7 +427,6 @@
         own_factors(t // ty + 1, lax.rem(t, ty) + 1)
         for code in range(9):
             make_weights(t, code)
-        apply_tile(t, first_rows)
 
         @pl.when(t == 3)
         def _():
@@ -439,6 +439,20 @@
         @pl.when(t == 11)
         def _():
             reduce_ss.finish()
+
+    @pl.loop(0, tiles)
+    def _(t):
+        @pl.when(inner(t))
+        def _():
+            apply_tile(t, first_rows)
+    halo_wait(vpad, v1_s, v1_r)
+    split_halo()
+
+    @pl.loop(0, tiles)
+    def _(t):
+        @pl.when(jnp.logical_not(inner(t)))
+        def _():
+            apply_tile(t, first_rows)
 
     def products(rows, extra):
         image[...] = jnp.zeros_like(image)
@@ -533,10 +547,6 @@
     cross = jnp.where(lane == rowi + prev, 1.0, cross)
     grams[prev : prev + width, :] = cross
     grams[:, prev : prev + width] = jnp.transpose(cross)
-
-    def inner(t):
-        a, b = t // ty, lax.rem(t, ty)
-        return (a >= 1) & (a < tx - 1) & (b >= 1) & (b < ty - 1)
 
     @pl.loop(0, tiles)
     def _(t):

time: 105 us -> 103 us (0.981)
  Pallas kernels: 99.4 us -> 97.6 us
    pallas_call x1, Pallas kernels: 99.4 us -> 97.6 us  [on_device(): pl.pallas_call(functools.partial(body, nsx, nsy, nsz, tx, ty), out_shape=...]
where the time goes in v4:
time: 103 us
  Pallas kernels  97.6 us (95%)
  local copies, waits for them, and re-layouts  4.85 us (5%)
    pallas_call x1, Pallas kernels, on_device(): pl.pallas_call(functools.partial(body, nsx, nsy, nsz, tx, ty), out_shape=...  97.6 us
    unnamed x5, local copies, waits for them, and re-layouts  4.85 us

profile of v4, /device:TPU:0, one launch (start us, length us, event | category | flops | bytes accessed | tf_op | source)
XLA Modules:
  0.0 103.1 jit_solution(15404822982716569848)
XLA Ops:
  0.6 1.4 %copy.6.links = s32[9,4,4]{2,1,0:T(4,128)} copy(s32[9,4,4]{0,2,1:T(4,128)} %param.7) | data formatting | bytes 1152 | tf_op args[3]
  2.0 97.6 %shard_map.59 = (f32[64,4,4,256]{3,2,1,0:T(4,128)}, f32[64,4,4,256]{3,2,1,0:T(4,128)}) custom-call(s32[9,4,4]{2,1,0:T(4,128)} %copy.6.links, f32[128,4,4,256]{3,2,1,0:T(4,128)} %prior_in.1, f32[64,4,4,256]{3,2,1,0:T(4,128)} %cur_in.1, f32[2,4,4,256]{3,2,1,0:T(4,128)} %pos_in.1), custom_call_target="tpu_custom_call" | custom-call | tf_op jit(solution)/shard_map/pallas_call | solution.py:619
  99.7 0.0 copy-start
  99.7 2.5 %copy.9 = f32[64,4,4,256]{3,2,1,0:T(4,128)} copy(f32[64,4,4,256]{3,2,1,0:T(4,128)} %get-tuple-element.4) | data formatting | bytes 2097152
  102.1 0.0 copy-done
  102.1 1.0 copy.10
Async XLA Ops:
  99.7 2.5 %copy-start = (f32[64,4,4,256]{3,2,1,0:T(4,128)S(1)}, f32[64,4,4,256]{3,2,1,0:T(4,128)}, u32[]{:S(2)}) copy-start(f32[64,4,4,256]{3,2,1,0:T(4,128)} %get-tuple-element.5) | copy-start | bytes 3145732

commit v5 on v3

--- a/solution.py
+++ b/solution.py
@@ -79,7 +79,7 @@
 
 
 def is_flat(nsx, nq):
-    return nsx * nq <= 16
+    return nsx * nq <= 4
 
 
 def body(

time: 105 us -> 101 us (0.962)
  Pallas kernels: 99.4 us -> 94.9 us
    pallas_call x1, Pallas kernels: 99.4 us -> 94.9 us  [on_device(): pl.pallas_call(functools.partial(body, nsx, nsy, nsz, tx, ty), out_shape=...]
where the time goes in v5:
time: 101 us; the launch traced here: 100 us
  Pallas kernels  94.9 us (94%)
  local copies, waits for them, and re-layouts  4.85 us (5%)
    pallas_call x1, Pallas kernels, on_device(): pl.pallas_call(functools.partial(body, nsx, nsy, nsz, tx, ty), out_shape=...  94.9 us
    unnamed x5, local copies, waits for them, and re-layouts  4.85 us

profile of v5, /device:TPU:0, one launch (start us, length us, event | category | flops | bytes accessed | tf_op | source)
XLA Modules:
  0.0 100.4 jit_solution(11010671026885672951)
XLA Ops:
  0.6 1.4 %copy.6.links = s32[9,4,4]{2,1,0:T(4,128)} copy(s32[9,4,4]{0,2,1:T(4,128)} %param.7) | data formatting | bytes 1152 | tf_op args[3]
  2.0 94.9 %shard_map.59 = (f32[64,4,4,256]{3,2,1,0:T(4,128)}, f32[64,4,4,256]{3,2,1,0:T(4,128)}) custom-call(s32[9,4,4]{2,1,0:T(4,128)} %copy.6.links, f32[128,4,4,256]{3,2,1,0:T(4,128)} %prior_in.1, f32[64,4,4,256]{3,2,1,0:T(4,128)} %cur_in.1, f32[2,4,4,256]{3,2,1,0:T(4,128)} %pos_in.1), custom_call_target="tpu_custom_call" | custom-call | tf_op jit(solution)/shard_map/pallas_call | solution.py:609
  97.0 0.0 copy-start
  97.0 2.5 %copy.9 = f32[64,4,4,256]{3,2,1,0:T(4,128)} copy(f32[64,4,4,256]{3,2,1,0:T(4,128)} %get-tuple-element.4) | data formatting | bytes 2097152
  99.4 0.0 copy-done
  99.4 1.0 copy.10
Async XLA Ops:
  97.0 2.5 %copy-start = (f32[64,4,4,256]{3,2,1,0:T(4,128)S(1)}, f32[64,4,4,256]{3,2,1,0:T(4,128)}, u32[]{:S(2)}) copy-start(f32[64,4,4,256]{3,2,1,0:T(4,128)} %get-tuple-element.5) | copy-start | bytes 3145732
